TPU v7x, 128 devices: a whole 4x4x4 slice. The times are simulated.
128 devices in a mesh: member: 16 (over z_lo, y, core), tile: 8 (over z_hi, x).
Axes of the slice: x: 4, y: 4, z: 4 (z_hi: 2, z_lo: 2; z = z_hi * 2 + z_lo), core: 2. Of those that a mesh axis runs over, the one named last changes fastest.
Arguments:
- node_fine: int32 [16, 12], P('member'), may hold values from 0 to 8
- node_coarse: int32 [64, 12], P('member'), may hold values from 0 to 8
- weight_fine: int32 [16], P('member'), may hold values from -3 to 3
- weight_coarse: int32 [64], P('member'), may hold values from -3 to 3
- mode_x: float32 [12, 128], replicated, may hold values from -1 to 1
- mode_y: float32 [12, 512], replicated, may hold values from -1 to 1
- mode_z: float32 [12, 32], replicated, may hold values from -1 to 1
- source_fine: float32 [128, 32, 512], P('tile'), may hold values from -12 to 12
- source_coarse: float32 [64, 16, 256], P(None, None, 'tile'), may hold values from -6 to 6
Outputs:
- combined: float32 [64, 16, 256], P('member', None, 'tile')
All inputs are finite; a program needn't handle non-finite values.
Results may differ from a plain program's by a relative error of at most 0.00026.
Values sent between devices are 32-bit elements; how exact they have to be, the bound alone decides.
A program may use at most 192 MiB of HBM per device.

v0:
```python
import math

import jax
import jax.numpy as jnp
from jax import lax
from jax.sharding import PartitionSpec as P

NODES = 9
SWEEPS = 3


CENTRE = 1.125
HALF_WIDTH = 0.875
SPREAD_RATIO = CENTRE / HALF_WIDTH


def extended(block, sides, width):
    for axis, dim in sides:
        count = lax.axis_size(axis)
        forward = [(i, i + 1) for i in range(count - 1)]
        backward = [(target, source) for source, target in forward]
        low = lax.ppermute(
            lax.slice_in_dim(block, block.shape[dim] - width, None, axis=dim), axis, forward
        )
        high = lax.ppermute(lax.slice_in_dim(block, 0, width, axis=dim), axis, backward)
        block = jnp.concatenate([low, block, high], axis=dim)
    return block


def sweep_factors(sweep_count):
    previous = 1.0 / SPREAD_RATIO
    factors = []
    for _ in range(sweep_count - 1):
        current = 1.0 / (2.0 * SPREAD_RATIO - previous)
        factors.append((current * previous, 2.0 * current / HALF_WIDTH))
        previous = current
    return factors


def shifted(tensor, spatial, along_dim, offset):
    for current in spatial:
        begin_at = offset if current == along_dim else 1
        tensor = lax.slice_in_dim(
            tensor, begin_at, tensor.shape[current] - 2 + begin_at, axis=current
        )
    return tensor


def diagonal_of(cond_pad, spatial):
    centre = shifted(cond_pad, spatial, -1, 1)
    running = jnp.zeros_like(centre)
    for along_dim in spatial:
        for offset in (0, 2):
            running = running + 0.5 * (centre + shifted(cond_pad, spatial, along_dim, offset))
    return running


def apply_op(field_pad, cond_pad, spatial):
    centre_k = shifted(cond_pad, spatial, -1, 1)
    centre_v = shifted(field_pad, spatial, -1, 1)
    running = jnp.zeros_like(centre_v * centre_k)
    for along_dim in spatial:
        for offset in (0, 2):
            coupling = 0.5 * (centre_k + shifted(cond_pad, spatial, along_dim, offset))
            running = running + coupling * (
                centre_v - shifted(field_pad, spatial, along_dim, offset)
            )
    return running


def node_values(node_index):
    return jnp.cos(math.pi * node_index.astype(jnp.float32) / (NODES - 1))


def pair_mean(modes):
    return 0.5 * (modes[:, 0::2] + modes[:, 1::2])


def log_field(values, along_x, along_z, along_y):
    weighted = (along_x.T * values)[:, None, :] * along_z.T[None, :, :]
    flattened = weighted.reshape(weighted.shape[0] * weighted.shape[1], weighted.shape[2])
    product = jnp.dot(flattened, along_y, precision=lax.Precision.HIGHEST)
    return product.reshape(weighted.shape[0], weighted.shape[1], along_y.shape[1])


def log_batch(values, along_x, along_z, along_y):
    weighted = (along_x.T[None, :, :] * values[:, None, :])[:, :, None, :] * along_z.T[
        None, None, :, :
    ]
    shape_in = weighted.shape
    flattened = weighted.reshape(shape_in[0] * shape_in[1] * shape_in[2], shape_in[3])
    product = jnp.dot(flattened, along_y, precision=lax.Precision.HIGHEST)
    return product.reshape(shape_in[0], shape_in[1], shape_in[2], along_y.shape[1])


def restrict(tensor):
    blocks = tensor.reshape(
        tensor.shape[0] // 2, 2, tensor.shape[1] // 2, 2, tensor.shape[2] // 2, 2
    )
    return blocks.sum(axis=(1, 3, 5)) * 0.125


def pad_other(tensor, halo_dim, spatial):
    widths = []
    for position in range(tensor.ndim):
        if position in spatial and position != halo_dim:
            widths.append((1, 1))
        else:
            widths.append((0, 0))
    return jnp.pad(tensor, widths)


def smooth_each(source, cond_pad, halo_dim, spatial, rim_fn, factors):
    diagonal = diagonal_of(cond_pad, spatial)
    update = source / (CENTRE * diagonal)
    result = update
    residual = source
    for keep_part, push_part in factors:
        field_pad = pad_other(rim_fn(update), halo_dim, spatial)
        residual = residual - apply_op(field_pad, cond_pad, spatial)
        update = keep_part * update + push_part * residual / diagonal
        result = result + update
    return result


def body(
    node_fine,
    node_coarse,
    weight_fine,
    weight_coarse,
    mode_x,
    mode_y,
    mode_z,
    source_fine,
    source_coarse,
):
    factors = sweep_factors(SWEEPS)
    tile_place = lax.axis_index("tile")
    strip_width = source_fine.shape[0]
    coarse_width = source_coarse.shape[2]
    mode_xc = pair_mean(mode_x)
    mode_yc = pair_mean(mode_y)
    mode_zc = pair_mean(mode_z)
    extent = 1
    padded_x = jnp.pad(mode_x, ((0, 0), (extent, extent)))
    mode_slab = lax.dynamic_slice_in_dim(
        padded_x, tile_place * strip_width, strip_width + 2 * extent, 1
    )
    global_x = (
        tile_place * strip_width - extent + jnp.arange(strip_width + 2 * extent, dtype=jnp.int32)
    )
    inside_x = ((global_x >= 0) & (global_x < mode_x.shape[1])).astype(jnp.float32)
    conduct = (
        jnp.exp(log_field(node_values(node_fine[0]), mode_slab, mode_z, mode_y))
        * inside_x[:, None, None]
    )
    cond_fine = pad_other(conduct, 0, (0, 1, 2))
    padded_y = jnp.pad(mode_yc, ((0, 0), (extent, extent)))
    mode_strip = lax.dynamic_slice_in_dim(
        padded_y, tile_place * coarse_width, coarse_width + 2 * extent, 1
    )
    global_y = (
        tile_place * coarse_width - extent + jnp.arange(coarse_width + 2 * extent, dtype=jnp.int32)
    )
    inside_y = ((global_y >= 0) & (global_y < mode_yc.shape[1])).astype(jnp.float32)
    conduct_c = (
        jnp.exp(log_batch(node_values(node_coarse), mode_xc, mode_zc, mode_strip)) * inside_y
    )
    cond_coarse = pad_other(conduct_c, 3, (1, 2, 3))

    def fine_rim(tensor):
        return extended(tensor, (("tile", 0),), 1)

    def coarse_rim(tensor):
        return extended(tensor, (("tile", 3),), 1)

    fine_result = smooth_each(source_fine, cond_fine, 0, (0, 1, 2), fine_rim, factors)
    coarse_result = smooth_each(source_coarse[None], cond_coarse, 3, (1, 2, 3), coarse_rim, factors)
    fine_part = weight_fine[0].astype(jnp.float32) * restrict(fine_result)
    arrived = lax.all_to_all(fine_part, "tile", split_axis=2, concat_axis=0, tiled=True)
    coarse_part = jnp.tensordot(
        weight_coarse.astype(jnp.float32), coarse_result, axes=1, precision=lax.Precision.HIGHEST
    )
    summed = arrived + coarse_part
    return lax.psum_scatter(summed, "member", scatter_dimension=0, tiled=True)


def solution(mesh):
    return jax.shard_map(
        body,
        mesh=mesh,
        in_specs=(
            P("member", None),
            P("member", None),
            P("member"),
            P("member"),
            P(),
            P(),
            P(),
            P("tile", None, None),
            P(None, None, "tile"),
        ),
        out_specs=P("member", None, "tile"),
        check_vma=False,
    )
```

profile of v0, /device:TPU:1, one launch (start us, length us, event | category | flops | bytes accessed | tf_op | source)
XLA Modules:
  0.0 244.2 jit_solution(13671199948675626248)
XLA Ops:
  6.5 0.9 slice.213
  7.4 0.9 slice.214
  8.3 1.2 slice.217
  9.6 1.2 slice.218
  13.3 1.4 fusion.6
  14.8 1.2 multiply_divide_fusion
  16.7 3.9 %collective-permute-start.4 = (f32[4,64,16,1]{1,3,2,0:T(1,128)}, f32[4,64,16,1]{1,3,2,0:T(1,128)S(1)}, u32[]{:S(2)}, u32[]{:S(2)}) collective-permute-start(f32[4,64,16,1]{1,3,2,0:T(1,128)} %get-tuple-element.19), channel_id=1, source_target_pairs={{0,1},{1,2},{2,3},{3,4},{4,5},{5,6},{6,7},{8,9},{9,10},{10,11},{11... | collective-permute-start | bytes 49160 | tf_op jit(solution)/shard_map/ppermute | solution.py:22
  20.6 1.3 collective-permute-start.5
  22.2 1.5 fusion.7
  23.7 0.9 multiply_divide_fusion.1
  24.6 0.8 collective-permute-done.5
  26.0 2.9 %divide_add_fusion = (f32[4,64,16,32]{1,3,2,0:T(8,128)S(1)}, f32[4,64,16,32]{1,3,2,0:T(8,128)S(1)}) fusion(f32[4,64,16,32]{1,3,2,0:T(8,128)S(1)} %get-tuple-element.12, f32[64,16,32]{0,2,1:T(8,128)S(1)} %copy-done.2, f32[4,64,16,32]{1,3,2,0:T(8,128)S(1)} %get-tuple-element.11, f32[4,64,16,1]{1,3,2,0:T(1,128)S(1)} %collective-permute-done.5, ...), kind=kLoop, calls=%fused_computation.148 | loop fusion | flops 4980736 | bytes 12124160 | tf_op jit(solution)/shard_map/add | solution.py:121
  29.0 3.5 %collective-permute-start.6 = (f32[4,64,16,1]{1,3,2,0:T(1,128)S(1)}, f32[4,64,16,1]{1,3,2,0:T(1,128)S(1)}, u32[]{:S(2)}, u32[]{:S(2)}) collective-permute-start(f32[4,64,16,1]{1,3,2,0:T(1,128)S(1)} %get-tuple-element.17), channel_id=1, source_target_pairs={{0,1},{1,2},{2,3},{3,4},{4,5},{5,6},{6,7},{8,9},{9,10},{10,11},{11... | collective-permute-start | bytes 49160 | tf_op jit(solution)/shard_map/ppermute | solution.py:22
  32.5 1.3 collective-permute-start.7
  33.8 5.1 %collective-permute-start = (f32[1,32,512]{2,1,0:T(8,128)S(1)}, f32[1,32,512]{2,1,0:T(8,128)S(1)}, u32[]{:S(2)}, u32[]{:S(2)}) collective-permute-start(f32[1,32,512]{2,1,0:T(8,128)S(1)} %get-tuple-element.15), channel_id=1, source_target_pairs={{0,1},{1,2},{2,3},{3,4},{4,5},{5,6},{6,7},{8,9},{9,10},{10,11},{11... | collective-permute-start | bytes 196616 | tf_op jit(solution)/shard_map/ppermute | solution.py:22
  39.0 1.3 collective-permute-start.1
  41.5 6.1 %collective-permute-done.1 = f32[1,32,512]{2,1,0:T(8,128)S(1)} collective-permute-done((f32[1,32,512]{2,1,0:T(8,128)S(1)}, f32[1,32,512]{2,1,0:T(8,128)S(1)}, u32[]{:S(2)}, u32[]{:S(2)}) %collective-permute-start.1) | collective-permute-done | bytes 65568 | tf_op jit(solution)/shard_map/ppermute | solution.py:25
  48.2 2.6 %divide_add_fusion.1 = (f32[16,32,512]{2,1,0:T(8,128)S(1)}, f32[16,32,512]{2,1,0:T(8,128)S(1)}) fusion(f32[16,32,512]{2,1,0:T(8,128)S(1)} %get-tuple-element.8, f32[16,32,512]{2,1,0:T(8,128)S(1)} %copy-done, f32[16,32,512]{2,1,0:T(8,128)S(1)} %get-tuple-element.7, f32[18,34,514]{2,1,0:T(8,128)S(1)} %select_maximum_fusion.2, f32[18,32,512]{2,1,0:T(8,128)S(1)} %fusion.7, ...), kind=kLoop, calls=%fused_computation.151 | loop fusion | flops 9961472 | bytes 13893632 | tf_op jit(solution)/shard_map/add | solution.py:121
  50.9 3.5 %collective-permute-start.2 = (f32[1,32,512]{2,1,0:T(8,128)S(1)}, f32[1,32,512]{2,1,0:T(8,128)S(1)}, u32[]{:S(2)}, u32[]{:S(2)}) collective-permute-start(f32[1,32,512]{2,1,0:T(8,128)S(1)} %get-tuple-element.13), channel_id=1, source_target_pairs={{0,1},{1,2},{2,3},{3,4},{4,5},{5,6},{6,7},{8,9},{9,10},{10,11},{11... | collective-permute-start | bytes 196616 | tf_op jit(solution)/shard_map/ppermute | solution.py:22
  54.4 1.5 collective-permute-start.3
  55.8 3.0 %fusion.31 = f32[4,64,16,32]{1,3,2,0:T(8,128)S(1)} fusion(f32[4,64,16,32]{1,3,2,0:T(8,128)S(1)} %get-tuple-element.12, f32[4,64,16,32]{1,3,2,0:T(8,128)S(1)} %get-tuple-element.10, f32[4,64,16,32]{1,3,2,0:T(8,128)S(1)} %get-tuple-element.9, f32[4,64,16,1]{1,3,2,0:T(1,128)S(1)} %collective-permute-done.7, f32[4,64,16,1]{1,3,2,0:T(1,128)S(1)} %collective-permute-done.6, ...), kind=kLoop, calls=%fused_computation.58 | loop fusion | flops 5242880 | bytes 12648448 | tf_op jit(solution)/shard_map/add | solution.py:122
  58.9 4.1 %collective-permute-done.3 = f32[1,32,512]{2,1,0:T(8,128)S(1)} collective-permute-done((f32[1,32,512]{2,1,0:T(8,128)S(1)}, f32[1,32,512]{2,1,0:T(8,128)S(1)}, u32[]{:S(2)}, u32[]{:S(2)}) %collective-permute-start.3) | collective-permute-done | bytes 65568 | tf_op jit(solution)/shard_map/ppermute | solution.py:25
  63.6 2.7 %fusion.64 = f32[16,32,512]{2,1,0:T(8,128)S(1)} fusion(f32[16,32,512]{2,1,0:T(8,128)S(1)} %get-tuple-element.8, f32[16,32,512]{2,1,0:T(8,128)S(1)} %get-tuple-element.6, f32[16,32,512]{2,1,0:T(8,128)S(1)} %get-tuple-element.5, f32[18,34,514]{2,1,0:T(8,128)S(1)} %select_maximum_fusion, f32[1,32,512]{2,1,0:T(8,128)S(1)} %collective-permute-done.3, ...), kind=kLoop, calls=%fused_computation.105 | loop fusion | flops 10485760 | bytes 13893632 | tf_op jit(solution)/shard_map/add | solution.py:122
  66.3 68.4 %reshape.40 = f32[8,2,16,2,256,2]{5,4,3,2,1,0:T(8,128)} reshape(f32[16,32,512]{2,1,0:T(8,128)S(1)} %fusion.64) | data formatting | bytes 2097152 | tf_op jit(solution)/shard_map/reshape | solution.py:97
  134.6 20.8 %reduce_sum.9 = f32[8,16,256]{2,1,0:T(8,128)S(1)} reduce(f32[8,2,16,2,256,2]{5,4,3,2,1,0:T(8,128)} %reshape.40, f32[]{:T(128)} %constant.18.clone.1), dimensions={1,3,5}, to_apply=%region_0.1 | reduce | flops 229376 | bytes 1179652 | tf_op jit(solution)/shard_map/reduce_sum | solution.py:100
  155.9 1.0 reshape.45
  156.9 10.6 %all-to-all-start = ((f32[8,1,4096]{2,1,0:T(1,128)}), f32[8,1,4096]{2,1,0:T(1,128)S(1)}, u32[]{:S(2)}, u32[]{:S(2)}) async-start(f32[8,1,4096]{2,1,0:T(1,128)} %reshape.45), calls=%async_computation | async-start | bytes 262144 | tf_op jit(solution)/shard_map/all_to_all | solution.py:180
  167.5 2.5 %fusion.92 = f32[1,64,16,32]{1,0,3,2:T(1,128)S(1)} fusion(f32[4,64,16,32]{1,3,2,0:T(8,128)S(1)} %fusion.31, s32[4]{0:T(128)S(1)} %copy-done.6), kind=kOutput, calls=%fused_computation.146 | convolution fusion | flops 1572868 | bytes 655376 | tf_op jit(solution)/shard_map/dot_general | solution.py:181
  170.3 4.1 %all-to-all-done = f32[8,1,4096]{2,1,0:T(1,128)S(1)} async-done(((f32[8,1,4096]{2,1,0:T(1,128)}), f32[8,1,4096]{2,1,0:T(1,128)S(1)}, u32[]{:S(2)}, u32[]{:S(2)}) %all-to-all-start) | async-done | bytes 131104 | tf_op jit(solution)/shard_map/all_to_all | solution.py:180
  174.9 1.0 reduce
  176.6 0.9 bitcast_add_fusion
  177.5 59.9 %reduce-scatter.2.cloned.1.call-done = f32[4,16,32]{2,1,0:T(8,128)} async-done(((f32[64,16,32]{2,1,0:T(8,128)}), f32[4,16,32]{2,1,0:T(8,128)}) %reduce-scatter.2.cloned.1.call-update) | async-done | bytes 8208 | tf_op jit(solution)/shard_map/reduce_scatter | solution.py:185
  (50 shorter events, 7.7 us)
Async XLA Ops:
  13.2 1.5 copy-start.1
  14.7 7.2 %copy-start.7 = (s32[1,12]{1,0:T(1,128)S(1)}, s32[1,12]{1,0:T(1,128)}, u32[]{:S(2)}) copy-start(s32[1,12]{1,0:T(1,128)} %param.9) | copy-start | bytes 148
  14.7 7.2 %copy-start.5 = (f32[12,128]{1,0:T(8,128)S(1)}, f32[12,128]{1,0:T(8,128)}, u32[]{:S(2)}) copy-start(f32[12,128]{1,0:T(8,128)} %param.13) | copy-start | bytes 18436
  14.7 7.4 %copy-start.3 = (f32[12,512]{1,0:T(8,128)S(1)}, f32[12,512]{1,0:T(8,128)}, u32[]{:S(2)}) copy-start(f32[12,512]{1,0:T(8,128)} %param.14) | copy-start | bytes 73732
  14.8 7.4 %copy-start.4 = (f32[12,32]{1,0:T(8,128)S(1)}, f32[12,32]{1,0:T(8,128)}, u32[]{:S(2)}) copy-start(f32[12,32]{1,0:T(8,128)} %param.15) | copy-start | bytes 4612
  16.7 8.0 %collective-permute-start.4 = (f32[4,64,16,1]{1,3,2,0:T(1,128)}, f32[4,64,16,1]{1,3,2,0:T(1,128)S(1)}, u32[]{:S(2)}, u32[]{:S(2)}) collective-permute-start(f32[4,64,16,1]{1,3,2,0:T(1,128)} %get-tuple-element.19), channel_id=1, source_target_pairs={{0,1},{1,2},{2,3},{3,4},{4,5},{5,6},{6,7},{8,9},{9,10},{10,11},{11... | collective-permute-start | bytes 49160 | tf_op jit(solution)/shard_map/ppermute | solution.py:22
  20.6 4.9 %collective-permute-start.5 = (f32[4,64,16,1]{1,3,2,0:T(1,128)}, f32[4,64,16,1]{1,3,2,0:T(1,128)S(1)}, u32[]{:S(2)}, u32[]{:S(2)}) collective-permute-start(f32[4,64,16,1]{1,3,2,0:T(1,128)} %get-tuple-element.20), channel_id=1, source_target_pairs={{1,0},{2,1},{3,2},{4,3},{5,4},{6,5},{7,6},{9,8},{10,9},{11,10},{12... | collective-permute-start | bytes 49160 | tf_op jit(solution)/shard_map/ppermute | solution.py:25
  22.2 1.5 copy-start
  24.6 1.4 copy-start.2
  29.0 11.9 %collective-permute-start.6 = (f32[4,64,16,1]{1,3,2,0:T(1,128)S(1)}, f32[4,64,16,1]{1,3,2,0:T(1,128)S(1)}, u32[]{:S(2)}, u32[]{:S(2)}) collective-permute-start(f32[4,64,16,1]{1,3,2,0:T(1,128)S(1)} %get-tuple-element.17), channel_id=1, source_target_pairs={{0,1},{1,2},{2,3},{3,4},{4,5},{5,6},{6,7},{8,9},{9,10},{10,11},{11... | collective-permute-start | bytes 49160 | tf_op jit(solution)/shard_map/ppermute | solution.py:22
  32.5 8.4 %collective-permute-start.7 = (f32[4,64,16,1]{1,3,2,0:T(1,128)S(1)}, f32[4,64,16,1]{1,3,2,0:T(1,128)S(1)}, u32[]{:S(2)}, u32[]{:S(2)}) collective-permute-start(f32[4,64,16,1]{1,3,2,0:T(1,128)S(1)} %get-tuple-element.18), channel_id=1, source_target_pairs={{1,0},{2,1},{3,2},{4,3},{5,4},{6,5},{7,6},{9,8},{10,9},{11,10},{12... | collective-permute-start | bytes 49160 | tf_op jit(solution)/shard_map/ppermute | solution.py:25
  33.8 7.7 %collective-permute-start = (f32[1,32,512]{2,1,0:T(8,128)S(1)}, f32[1,32,512]{2,1,0:T(8,128)S(1)}, u32[]{:S(2)}, u32[]{:S(2)}) collective-permute-start(f32[1,32,512]{2,1,0:T(8,128)S(1)} %get-tuple-element.15), channel_id=1, source_target_pairs={{0,1},{1,2},{2,3},{3,4},{4,5},{5,6},{6,7},{8,9},{9,10},{10,11},{11... | collective-permute-start | bytes 196616 | tf_op jit(solution)/shard_map/ppermute | solution.py:22
  39.0 8.6 %collective-permute-start.1 = (f32[1,32,512]{2,1,0:T(8,128)S(1)}, f32[1,32,512]{2,1,0:T(8,128)S(1)}, u32[]{:S(2)}, u32[]{:S(2)}) collective-permute-start(f32[1,32,512]{2,1,0:T(8,128)S(1)} %get-tuple-element.16), channel_id=1, source_target_pairs={{1,0},{2,1},{3,2},{4,3},{5,4},{6,5},{7,6},{9,8},{10,9},{11,10},{12... | collective-permute-start | bytes 196616 | tf_op jit(solution)/shard_map/ppermute | solution.py:25
  50.9 8.0 %collective-permute-start.2 = (f32[1,32,512]{2,1,0:T(8,128)S(1)}, f32[1,32,512]{2,1,0:T(8,128)S(1)}, u32[]{:S(2)}, u32[]{:S(2)}) collective-permute-start(f32[1,32,512]{2,1,0:T(8,128)S(1)} %get-tuple-element.13), channel_id=1, source_target_pairs={{0,1},{1,2},{2,3},{3,4},{4,5},{5,6},{6,7},{8,9},{9,10},{10,11},{11... | collective-permute-start | bytes 196616 | tf_op jit(solution)/shard_map/ppermute | solution.py:22
  54.4 8.6 %collective-permute-start.3 = (f32[1,32,512]{2,1,0:T(8,128)S(1)}, f32[1,32,512]{2,1,0:T(8,128)S(1)}, u32[]{:S(2)}, u32[]{:S(2)}) collective-permute-start(f32[1,32,512]{2,1,0:T(8,128)S(1)} %get-tuple-element.14), channel_id=1, source_target_pairs={{1,0},{2,1},{3,2},{4,3},{5,4},{6,5},{7,6},{9,8},{10,9},{11,10},{12... | collective-permute-start | bytes 196616 | tf_op jit(solution)/shard_map/ppermute | solution.py:25
  155.4 12.1 %copy-start.6 = (s32[4]{0:T(128)S(1)}, s32[4]{0:T(128)}, u32[]{:S(2)}) copy-start(s32[4]{0:T(128)} %param.12) | copy-start | bytes 52
  156.9 17.5 %all-to-all-start = ((f32[8,1,4096]{2,1,0:T(1,128)}), f32[8,1,4096]{2,1,0:T(1,128)S(1)}, u32[]{:S(2)}, u32[]{:S(2)}) async-start(f32[8,1,4096]{2,1,0:T(1,128)} %reshape.45), calls=%async_computation | async-start | bytes 262144 | tf_op jit(solution)/shard_map/all_to_all | solution.py:180
  167.5 69.9 %reduce-scatter.2.cloned.1.call-start = ((), (), s32[]{:S(2)}) async-start(), calls=%async_computation.2 | async-start | bytes 557056 | tf_op jit(solution)/shard_map/reduce_scatter | solution.py:185
Sparse Core Ops, SparseCore 0:
  177.6 59.7 reduce-scatter.1
where the time goes:
time: 248 us; the launch traced here: 244 us
  local copies, waits for them, and re-layouts  78.1 us (31%)
  waiting for transfers between devices  75 us (30%)
  other arithmetic  39.2 us (16%)
  starting transfers between devices  32 us (13%)
  between operations  14.5 us (6%)
  matrix products  5.35 us (2%)
    reshape x1, local copies, waits for them, and re-layouts, restrict(): tensor.reshape(tensor.shape[0] // 2, 2, tensor.shape[1] // 2, 2, tensor.s...  68.4 us
    reduce_scatter x1, waiting for transfers between devices, body(): return lax.psum_scatter(summed, 'member', scatter_dimension=0, tiled=True)  59.9 us
    reduce_sum x1, other arithmetic, restrict(): return blocks.sum(axis=(1, 3, 5)) * 0.125  20.8 us
    ppermute x4, starting transfers between devices, extended(): lax.ppermute(lax.slice_in_dim(block, block.shape[dim] - width, None, axis...  16.1 us
    ppermute x4, waiting for transfers between devices, extended(): lax.ppermute(lax.slice_in_dim(block, 0, width, axis=dim), axis, backward)  11 us
    all_to_all x1, starting transfers between devices, body(): lax.all_to_all(fine_part, 'tile', split_axis=2, concat_axis=0, tiled=True)  10.6 us
    slice x6, local copies, waits for them, and re-layouts, pair_mean(): return 0.5 * (modes[:, 0::2] + modes[:, 1::2])  5.84 us
    add x2, other arithmetic, smooth_each(): result = result + update  5.74 us
  transfers between devices with their start and end apart: 10, of which 5 were waited for; matrix products, arithmetic and copies ran while one was open for 4% of the time, Pallas kernels for 0%

commit v1 on v0

v1 whole, which is shorter than its diff:
```python
import math

import jax
import jax.numpy as jnp
from jax import lax
from jax.experimental import pallas as pl
from jax.experimental.pallas import tpu as pltpu
from jax.sharding import PartitionSpec as P

NODES = 9
SWEEPS = 3
CENTRE = 1.125
HALF_WIDTH = 0.875
SPREAD_RATIO = CENTRE / HALF_WIDTH
LOG2E = 1.0 / math.log(2.0)

F32 = jnp.float32
BF16 = jnp.bfloat16
MESH = pl.DeviceIdType.MESH

TILES = 8
MEMBERS = 16
KL = 12
KP = 16
XS = 16
XC = 8
XPAD = 8


def sweep_factors(sweep_count):
    previous = 1.0 / SPREAD_RATIO
    factors = []
    for _ in range(sweep_count - 1):
        current = 1.0 / (2.0 * SPREAD_RATIO - previous)
        factors.append((current * previous, 2.0 * current / HALF_WIDTH))
        previous = current
    return factors


(KEEP1, PUSH1), (KEEP2, PUSH2) = sweep_factors(SWEEPS)
FIRST = 1.0 / CENTRE


def iota(shape, dim):
    return lax.broadcasted_iota(jnp.int32, shape, dim)


def halves(value):
    high = value.astype(BF16)
    return high, (value - high.astype(F32)).astype(BF16)


def thirds(value):
    high = value.astype(BF16)
    rest = value - high.astype(F32)
    middle = rest.astype(BF16)
    return high, middle, (rest - middle.astype(F32)).astype(BF16)


def stencil(below, here, above, masks):
    lane_first, lane_last, sub_first, sub_last = masks
    dims = here.ndim
    ka, ja, sa, la = dims - 4, dims - 3, dims - 2, dims - 1
    nk, nj = here.shape[ka], here.shape[ja]

    def part(low, high, axis):
        return lax.slice_in_dim(here, low, high, axis=axis)

    k_wrap = jnp.where(lane_first, 0.0, pltpu.roll(part(nk - 1, nk, ka), 1, la))
    k_down = jnp.concatenate([k_wrap, part(0, nk - 1, ka)], ka)
    k_wrap = jnp.where(lane_last, 0.0, pltpu.roll(part(0, 1, ka), 127, la))
    k_up = jnp.concatenate([part(1, nk, ka), k_wrap], ka)
    j_wrap = jnp.where(sub_first, 0.0, pltpu.roll(part(nj - 1, nj, ja), 1, sa))
    j_down = jnp.concatenate([j_wrap, part(0, nj - 1, ja)], ja)
    j_wrap = jnp.where(sub_last, 0.0, pltpu.roll(part(0, 1, ja), 7, sa))
    j_up = jnp.concatenate([part(1, nj, ja), j_wrap], ja)
    return ((below + above) + (k_down + k_up)) + (j_down + j_up)


def node_column(node_row):
    index = node_row
    value = jnp.zeros(node_row.shape, F32)
    for node in range(NODES):
        value = jnp.where(index == node, math.cos(math.pi * node / (NODES - 1)) * LOG2E, value)
    spread = jnp.broadcast_to(value, (KP, KL))
    own = iota((KP, KL), 0) == iota((KP, KL), 1)
    return jnp.sum(jnp.where(own, spread, 0.0), axis=1, keepdims=True)


def block_transpose(blocks, width, lanes):
    count = len(blocks)
    place = lanes // width
    blocks = list(blocks)
    bit = 1
    while bit < count:
        clear = (place & bit) == 0
        for low in range(count):
            if low & bit:
                continue
            a, b = blocks[low], blocks[low | bit]
            blocks[low] = jnp.where(clear, a, pltpu.roll(b, width * bit, 1))
            blocks[low | bit] = jnp.where(clear, pltpu.roll(a, 128 - width * bit, 1), b)
        bit *= 2
    return blocks


def kernel(
    node_f,
    node_c,
    w_f,
    w_c,
    mode_x,
    mode_y,
    mode_z,
    src_f,
    src_c,
    out,
    fraw,
    craw,
    cpack,
    cgot,
    mpad,
    xt,
    zt,
    perm_f,
    perm_c,
    rhs_f,
    rhs_c,
    logs_f,
    logs_c,
    c_f,
    f_f,
    inv_f,
    d_f,
    w0_f,
    e_f,
    w1_f,
    a_f,
    u_f,
    c_c,
    f_c,
    inv_c,
    d_c,
    w0_c,
    e_c,
    w1_c,
    a_c,
    u_c,
    tot,
    sendbuf,
    recvbuf,
    local_sem,
    halo_send,
    halo_recv,
    cs_send,
    cs_recv,
    fin_send,
    fin_recv,
):
    me_m = lax.axis_index("member")
    me_t = lax.axis_index("tile")

    def to(member, tile):
        return {"member": member, "tile": tile}

    barrier = pltpu.get_barrier_semaphore()
    for step in range(1, TILES):
        pl.semaphore_signal(
            barrier,
            inc=1,
            device_id=to(me_m, lax.rem(me_t + step, TILES)),
            device_id_type=MESH,
        )
    feeding_tile = me_m // 2
    for source in range(MEMBERS):

        @pl.when(jnp.logical_not((source == me_m) & (feeding_tile == me_t)))
        def _():
            pl.semaphore_signal(
                barrier, inc=1, device_id=to(source, feeding_tile), device_id_type=MESH
            )

    own_c = pltpu.make_async_copy(src_c, craw, local_sem.at[4])
    own_c.start()
    own_f = []
    for q in range(4):
        copy = pltpu.make_async_copy(
            src_f.at[:, :, pl.ds(128 * q, 128)], fraw.at[pl.ds(2, XS), q], local_sem.at[q]
        )
        copy.start()
        own_f.append(copy)

    lanes = iota((8, 128), 1)
    subs = iota((8, 128), 0)
    masks = (lanes == 0, lanes == 127, subs == 0, subs == 7)

    own_c.wait()
    cpack[0] = jnp.zeros((8, 128), F32)
    cpack[33] = jnp.zeros((8, 128), F32)

    def pack(pair, carry):
        cpack[pair + 1] = jnp.concatenate(
            [craw[2 * pair + a, pl.ds(j, 8, stride=2), :] for a in range(2) for j in range(2)], 1
        )
        return carry

    lax.fori_loop(0, 32, pack, 0, unroll=4)

    pl.semaphore_wait(barrier, 23 - (feeding_tile == me_t).astype(jnp.int32))

    has_left = me_t > 0
    has_right = me_t < TILES - 1

    def halo_copy(q, rightwards):
        if rightwards:
            return pltpu.make_async_remote_copy(
                src_ref=src_f.at[pl.ds(XS - 2, 2), :, pl.ds(128 * q, 128)],
                dst_ref=fraw.at[pl.ds(0, 2), q],
                send_sem=halo_send.at[q],
                recv_sem=halo_recv.at[q],
                device_id=to(me_m, lax.rem(me_t + 1, TILES)),
                device_id_type=MESH,
            )
        return pltpu.make_async_remote_copy(
            src_ref=src_f.at[pl.ds(0, 2), :, pl.ds(128 * q, 128)],
            dst_ref=fraw.at[pl.ds(XS + 2, 2), q],
            send_sem=halo_send.at[4 + q],
            recv_sem=halo_recv.at[4 + q],
            device_id=to(me_m, lax.rem(me_t + TILES - 1, TILES)),
            device_id_type=MESH,
        )

    @pl.when(has_right)
    def _():
        for q in range(4):
            halo_copy(q, True).start()

    @pl.when(has_left)
    def _():
        for q in range(4):
            halo_copy(q, False).start()

    @pl.when(jnp.logical_not(has_left))
    def _():
        fraw[0:2] = jnp.zeros((2, 4, 32, 128), F32)

    @pl.when(jnp.logical_not(has_right))
    def _():
        fraw[XS + 2 : XS + 4] = jnp.zeros((2, 4, 32, 128), F32)

    def strip_copy(step):
        there = lax.rem(me_t + step, TILES)
        return pltpu.make_async_remote_copy(
            src_ref=cpack.at[pl.ds(4 * there, 6)],
            dst_ref=cgot.at[me_t],
            send_sem=cs_send.at[step],
            recv_sem=cs_recv.at[step],
            device_id=to(me_m, there),
            device_id_type=MESH,
        )

    for step in range(1, TILES):
        strip_copy(step).start()
    cgot[me_t] = cpack[pl.ds(4 * me_t, 6)]

    col = iota((512, 512), 1)
    match = iota((512, 512), 0) == 4 * (col & 127) + (col >> 7)
    moved = jnp.where(match, 2.0, 0.0).astype(BF16)
    perm_f[0:512] = moved
    perm_f[512:1024] = moved
    col = iota((256, 256), 1)
    match = iota((256, 256), 0) == 2 * (col & 127) + (col >> 7)
    moved = jnp.where(match, 2.0, 0.0).astype(BF16)
    perm_c[0:256] = moved
    perm_c[256:512] = moved

    mpad[...] = jnp.zeros(mpad.shape, F32)
    mpad[0:KL, :] = mode_y[...]
    my_parts = thirds(mpad[...])
    my = 0.5 * sum(
        jnp.dot(part, perm_f[0:512], preferred_element_type=F32) for part in my_parts
    )
    mpad[0:KL, 0:128] = mode_x[...]
    stacked = jnp.concatenate([mpad[:, 0:128]] * 8, 0)
    xt[...] = jnp.zeros(xt.shape, F32)
    xt[XPAD : XPAD + 128, :] = stacked.T
    mpad[0:KL, 0:32] = mode_z[...]
    stacked = jnp.concatenate([mpad[:, 0:32]] * 8, 0)
    zt[...] = stacked.T
    zf = [zt[pl.ds(j, 8, stride=4), :] for j in range(4)]
    zc = [0.5 * (zf[2 * j] + zf[2 * j + 1]) for j in range(2)]
    zf = jnp.concatenate(zf, 0)
    zc = jnp.concatenate(zc, 0)

    def sides(value):
        high, low = halves(value)
        return jnp.concatenate([high, low, high, low], 0)

    rhs_f[...] = jnp.zeros(rhs_f.shape, BF16)
    rhs_c[...] = jnp.zeros(rhs_c.shape, BF16)
    rhs_f[0:64, :] = sides(my * node_column(node_f[...]))
    myc = jnp.concatenate(
        [0.5 * (my[:, 256 * k : 256 * k + 128] + my[:, 256 * k + 128 : 256 * k + 256]) for k in range(2)], 1
    )
    for m in range(4):
        rhs_c[0:64, 256 * m : 256 * m + 256] = sides(myc * node_column(node_c[m : m + 1, :]))

    def left(value):
        high = value.astype(BF16).astype(F32)
        group = iota(value.shape, 1)
        return jnp.where(group < 32, high, value - high).astype(BF16)

    x0 = me_t * XS

    rows = []
    for i in range(XS + 6):
        rows.append(left(xt[pl.ds(x0 - 3 + XPAD + i, 1), :] * zf))
    logs_f[...] = jnp.dot(
        jnp.concatenate(rows, 0), rhs_f[...], preferred_element_type=F32
    )

    def cond_fine(i, carry):
        x = x0 - 3 + i
        inside = ((x >= 0) & (x < XS * TILES)).astype(F32)
        base = pl.multiple_of(i * 32, 32)
        for k in range(4):
            for j in range(4):
                c_f[i, k, j] = (
                    jnp.exp2(logs_f[pl.ds(base + 8 * j, 8), 128 * k : 128 * k + 128]) * inside
                )
        return carry

    lax.fori_loop(0, XS + 6, cond_fine, 0)

    rows = []
    for i in range(XC + 6):
        at = x0 - 6 + XPAD + 2 * i
        mean = 0.5 * (xt[pl.ds(at, 1), :] + xt[pl.ds(at + 1, 1), :])
        rows.append(left(mean * zc))
    logs_c[...] = jnp.dot(
        jnp.concatenate(rows, 0), rhs_c[...], preferred_element_type=F32
    )

    xc0 = me_t * XC

    def cond_coarse(i, carry):
        x = xc0 - 3 + i
        inside = ((x >= 0) & (x < XC * TILES)).astype(F32)
        base = pl.multiple_of(i * 16, 16)
        for m in range(4):
            for k in range(2):
                for j in range(2):
                    at = 256 * m + 128 * k
                    c_c[i, m, k, j] = (
                        jnp.exp2(logs_c[pl.ds(base + 8 * j, 8), at : at + 128]) * inside
                    )
        return carry

    lax.fori_loop(0, XC + 6, cond_coarse, 0)

    for copy in own_f:
        copy.wait()

    @pl.when(has_left)
    def _():
        for q in range(4):
            halo_copy(q, True).wait_recv()

    @pl.when(has_right)
    def _():
        for q in range(4):
            halo_copy(q, False).wait_recv()

    def source_fine(chunk, carry):
        rows = []
        for i in range(5):
            for j in range(4):
                rows.append(
                    jnp.concatenate(
                        [fraw[5 * chunk + i, q, pl.ds(j, 8, stride=4), :] for q in range(4)], 1
                    )
                )
        high, low = halves(jnp.concatenate(rows, 0))
        got = jnp.dot(
            jnp.concatenate([high, low], 1), perm_f[...], preferred_element_type=F32
        )
        for i in range(5):
            for k in range(4):
                for j in range(4):
                    f_f[5 * chunk + i, k, j] = got[
                        32 * i + 8 * j : 32 * i + 8 * j + 8, 128 * k : 128 * k + 128
                    ]
        return carry

    lax.fori_loop(0, 4, source_fine, 0)

    def start(i, offset, x_first, x_count, c, f, inv, d, w0, fine):
        x = x_first + i
        inside = (x >= 0) & (x < x_count)
        here = c[i + 1]
        total = 6.0 * here + stencil(c[i], here, c[i + 2], masks)
        turned = pltpu.reciprocal(total, approx=True)
        turned = turned * (2.0 - total * turned)
        turned = jnp.where(inside, turned, 0.0)
        inv[i] = turned
        source = f[i] if fine else f[i][None]
        first = (FIRST * source) * turned
        d[i] = first
        w0[i] = here * first

    def middle(i, c, f, inv, d, w0, e, w1, a, u, fine):
        source = f[i + 1] if fine else f[i + 1][None]
        here, prev = c[i + 2], d[i + 1]
        push = here * stencil(d[i], prev, d[i + 2], masks) + stencil(
            w0[i], w0[i + 1], w0[i + 2], masks
        )
        residual = (1.0 - FIRST) * source + push
        step = KEEP1 * prev + PUSH1 * (residual * inv[i + 1])
        e[i] = step
        w1[i] = here * step
        a[i] = (1.0 - PUSH1) * residual - (KEEP1 * FIRST) * source
        u[i] = prev + (1.0 + KEEP2) * step

    def finish(i, c, inv, e, w1, a, u):
        here = c[i + 3]
        push = here * stencil(e[i], e[i + 1], e[i + 2], masks) + stencil(
            w1[i], w1[i + 1], w1[i + 2], masks
        )
        residual = a[i + 1] + push
        return u[i + 1] + PUSH2 * (residual * inv[i + 2])

    def start_fine(i, carry):
        start(i, 0, x0 - 2, XS * TILES, c_f, f_f, inv_f, d_f, w0_f, True)
        return carry

    lax.fori_loop(0, XS + 4, start_fine, 0)

    def middle_fine(i, carry):
        middle(i, c_f, f_f, inv_f, d_f, w0_f, e_f, w1_f, a_f, u_f, True)
        return carry

    lax.fori_loop(0, XS + 2, middle_fine, 0)

    for step in range(1, TILES):
        strip_copy(step).wait_recv()
    rows = []
    for pair in range(6):
        sides_of = [
            block_transpose([cgot[4 * half + q, pair] for q in range(4)], 32, lanes)
            for half in range(2)
        ]
        for g in range(4):
            rows.append(jnp.concatenate([sides_of[0][g], sides_of[1][g]], 1))
    high, low = halves(jnp.concatenate(rows, 0))
    got = jnp.dot(jnp.concatenate([high, low], 1), perm_c[...], preferred_element_type=F32)
    for i in range(XC + 4):
        for k in range(2):
            for j in range(2):
                at = 16 * i + 8 * j
                f_c[i, k, j] = got[at : at + 8, 128 * k : 128 * k + 128]

    def start_coarse(i, carry):
        start(i, 0, xc0 - 2, XC * TILES, c_c, f_c, inv_c, d_c, w0_c, False)
        return carry

    lax.fori_loop(0, XC + 4, start_coarse, 0)

    def middle_coarse(i, carry):
        middle(i, c_c, f_c, inv_c, d_c, w0_c, e_c, w1_c, a_c, u_c, False)
        return carry

    lax.fori_loop(0, XC + 2, middle_coarse, 0)

    weight_f = w_f[0].astype(F32) * 0.125
    weight_c = [w_c[m].astype(F32) for m in range(4)]

    def finish_plane(xc, carry):
        pair = finish(2 * xc, c_f, inv_f, e_f, w1_f, a_f, u_f) + finish(
            2 * xc + 1, c_f, inv_f, e_f, w1_f, a_f, u_f
        )
        coarse = finish(xc, c_c, inv_c, e_c, w1_c, a_c, u_c)
        for k in range(2):
            for j in range(2):
                block = (pair[2 * k, 2 * j] + pair[2 * k + 1, 2 * j]) + (
                    pair[2 * k, 2 * j + 1] + pair[2 * k + 1, 2 * j + 1]
                )
                block = weight_f * block
                for m in range(4):
                    block = block + weight_c[m] * coarse[m, k, j]
                tot[xc, k, j] = block
        return carry

    def piece_copy(e, t):
        return pltpu.make_async_remote_copy(
            src_ref=sendbuf.at[e, t],
            dst_ref=recvbuf.at[me_m],
            send_sem=fin_send.at[e, t],
            recv_sem=fin_recv.at[me_m],
            device_id=to(2 * me_t + e, t),
            device_id_type=MESH,
        )

    def is_own(e, t):
        return (me_m == 2 * me_t + e) & (me_t == t)

    for e in range(2):
        lax.fori_loop(4 * e, 4 * e + 4, finish_plane, 0)
        for chi in range(2):
            pieces = block_transpose(
                [
                    tot[4 * e + 2 * chi + a, k, j]
                    for a in range(2)
                    for j in range(2)
                    for k in range(2)
                ],
                16,
                lanes,
            )
            for t in range(TILES):
                sendbuf[e, t, chi] = pieces[t]
        for t in range(TILES):

            @pl.when(is_own(e, t))
            def _():
                recvbuf[me_m] = sendbuf[e, t]

            @pl.when(jnp.logical_not(is_own(e, t)))
            def _():
                piece_copy(e, t).start()

    @pl.when(has_right)
    def _():
        for q in range(4):
            halo_copy(q, True).wait_send()

    @pl.when(has_left)
    def _():
        for q in range(4):
            halo_copy(q, False).wait_send()

    for step in range(1, TILES):
        strip_copy(step).wait_send()

    for source in range(MEMBERS):

        @pl.when(jnp.logical_not((source == me_m) & (feeding_tile == me_t)))
        def _():
            pltpu.make_async_remote_copy(
                src_ref=sendbuf.at[0, 0],
                dst_ref=recvbuf.at[source],
                send_sem=fin_send.at[0, 0],
                recv_sem=fin_recv.at[source],
                device_id=to(source, feeding_tile),
                device_id_type=MESH,
            ).wait_recv()

    total = recvbuf[0]
    for source in range(1, MEMBERS):
        total = total + recvbuf[source]
    row = iota((128, 128), 0)
    colm = iota((128, 128), 1)
    target = (row & 96) + 2 * (row & 15) + ((row >> 4) & 1)
    order = jnp.where(target == colm, 1.0, 0.0).astype(BF16)
    flat = total.reshape(16, 128)
    flat = sum(jnp.dot(part, order, preferred_element_type=F32) for part in thirds(flat))
    for chi in range(2):
        for g in range(4):
            out[2 * chi + g // 2, pl.ds(g % 2, 8, stride=2), :] = flat[
                8 * chi : 8 * chi + 8, 32 * g : 32 * g + 32
            ]

    for e in range(2):
        for t in range(TILES):

            @pl.when(jnp.logical_not(is_own(e, t)))
            def _():
                piece_copy(e, t).wait_send()


def body(*args):
    vmem = pl.BlockSpec(memory_space=pltpu.VMEM)
    smem = pl.BlockSpec(memory_space=pltpu.SMEM)
    hbm = pl.BlockSpec(memory_space=pl.ANY)
    fine = (4, 4, 8, 128)
    flat = (2, 2, 8, 128)
    coarse = (4, 2, 2, 8, 128)
    dma = pltpu.SemaphoreType.DMA
    scratch = [
        pltpu.VMEM((XS + 4, 4, 32, 128), F32),
        pltpu.VMEM((64, 16, 32), F32),
        pltpu.VMEM((34, 8, 128), F32),
        pltpu.VMEM((TILES, 6, 8, 128), F32),
        pltpu.VMEM((KP, 512), F32),
        pltpu.VMEM((XPAD + 128 + XPAD, 128), F32),
        pltpu.VMEM((32, 128), F32),
        pltpu.VMEM((1024, 512), BF16),
        pltpu.VMEM((512, 256), BF16),
        pltpu.VMEM((128, 512), BF16),
        pltpu.VMEM((128, 1024), BF16),
        pltpu.VMEM(((XS + 6) * 32, 512), F32),
        pltpu.VMEM(((XC + 6) * 16, 1024), F32),
        pltpu.VMEM((XS + 6,) + fine, F32),
        pltpu.VMEM((XS + 4,) + fine, F32),
        pltpu.VMEM((XS + 4,) + fine, F32),
        pltpu.VMEM((XS + 4,) + fine, F32),
        pltpu.VMEM((XS + 4,) + fine, F32),
        pltpu.VMEM((XS + 2,) + fine, F32),
        pltpu.VMEM((XS + 2,) + fine, F32),
        pltpu.VMEM((XS + 2,) + fine, F32),
        pltpu.VMEM((XS + 2,) + fine, F32),
        pltpu.VMEM((XC + 6,) + coarse, F32),
        pltpu.VMEM((XC + 4,) + flat, F32),
        pltpu.VMEM((XC + 4,) + coarse, F32),
        pltpu.VMEM((XC + 4,) + coarse, F32),
        pltpu.VMEM((XC + 4,) + coarse, F32),
        pltpu.VMEM((XC + 2,) + coarse, F32),
        pltpu.VMEM((XC + 2,) + coarse, F32),
        pltpu.VMEM((XC + 2,) + coarse, F32),
        pltpu.VMEM((XC + 2,) + coarse, F32),
        pltpu.VMEM((XC,) + flat, F32),
        pltpu.VMEM((2, TILES, 2, 8, 128), F32),
        pltpu.VMEM((MEMBERS, 2, 8, 128), F32),
        dma((5,)),
        dma((8,)),
        dma((8,)),
        dma((TILES,)),
        dma((TILES,)),
        dma((2, TILES)),
        dma((MEMBERS,)),
    ]
    return pl.pallas_call(
        kernel,
        out_shape=jax.ShapeDtypeStruct((4, 16, 32), F32),
        in_specs=[vmem, vmem, smem, smem, vmem, vmem, vmem, hbm, hbm],
        out_specs=vmem,
        scratch_shapes=scratch,
        compiler_params=pltpu.CompilerParams(
            collective_id=0, has_side_effects=True, vmem_limit_bytes=48 * 2**20
        ),
    )(*args)


def solution(mesh):
    return jax.shard_map(
        body,
        mesh=mesh,
        in_specs=(
            P("member", None),
            P("member", None),
            P("member"),
            P("member"),
            P(),
            P(),
            P(),
            P("tile", None, None),
            P(None, None, "tile"),
        ),
        out_specs=P("member", None, "tile"),
        check_vma=False,
    )
```

time: 248 us -> 34.3 us (0.14)
  the two profiles are of different devices: /device:TPU:1 before, /device:TPU:37 now
where the time goes in v1:
time: 34.3 us; the launch traced here: 34.2 us
  Pallas kernels  30.3 us (88%)
  local copies, waits for them, and re-layouts  3.13 us (9%)
  between operations  0.77 us (2%)
    pallas_call x1, Pallas kernels, body(): pl.pallas_call(kernel, out_shape=jax.ShapeDtypeStruct((4, 16, 32), F32),...  30.3 us
    unnamed x16, local copies, waits for them, and re-layouts  3.13 us

profile of v1, /device:TPU:37, one launch (start us, length us, event | category | flops | bytes accessed | tf_op | source)
XLA Modules:
  0.0 34.2 jit_solution(14981679059691576682)
XLA Ops:
  0.7 0.0 copy-start.1
  0.7 0.0 copy-start.2
  0.7 0.0 copy-start.3
  0.7 0.0 copy-start.4
  0.7 0.0 copy-start.5
  0.7 0.0 copy-start.6
  0.7 1.3 %copy.10.src_c = f32[64,16,32]{2,1,0:T(8,128)S(1)} copy(f32[64,16,32]{0,2,1:T(8,128)} %param.17) | data formatting | bytes 262144 | tf_op args[8]
  2.0 0.0 copy-done.1
  2.0 0.0 copy-done.2
  2.0 0.0 copy-done.3
  2.0 0.0 copy-done.4
  2.0 0.0 copy-done.5
  2.0 0.0 copy-done.6
  2.0 0.0 copy-start
  2.1 1.2 %copy-done = f32[16,32,512]{2,1,0:T(8,128)S(1)} copy-done((f32[16,32,512]{2,1,0:T(8,128)S(1)}, f32[16,32,512]{2,1,0:T(8,128)}, u32[]{:S(2)}) %copy-start) | copy-done | bytes 1048600
  3.3 30.3 %shard_map.91 = f32[4,16,32]{2,1,0:T(8,128)S(1)} custom-call(s32[1,12]{1,0:T(1,128)S(1)} %copy-done.5, s32[4,12]{1,0:T(4,128)S(1)} %copy-done.4, s32[1]{0:T(128)S(6)} %copy.12.w_f, s32[4]{0:T(128)S(1)} %copy-done.6, f32[12,128]{1,0:T(8,128)S(1)} %copy-done.2, f32[12,512]{1,0:T(8,128)S(1)} %copy-done.1, f32[12,32]{1,0:T(8,128)S(1)} %copy-done.3, ...), custom_call_target="tpu_custom_call" | custom-call | tf_op jit(solution)/shard_map/pallas_call | solution.py:631
  33.6 0.6 %copy.13 = f32[4,16,32]{2,1,0:T(8,128)} copy(f32[4,16,32]{2,1,0:T(8,128)S(1)} %shard_map.91) | data formatting | bytes 16384
Async XLA Ops:
  0.7 1.3 %copy-start.1 = (f32[12,512]{1,0:T(8,128)S(1)}, f32[12,512]{1,0:T(8,128)}, u32[]{:S(2)}) copy-start(f32[12,512]{1,0:T(8,128)} %mode_y.1) | copy-start | bytes 73732
  0.7 1.3 %copy-start.2 = (f32[12,128]{1,0:T(8,128)S(1)}, f32[12,128]{1,0:T(8,128)}, u32[]{:S(2)}) copy-start(f32[12,128]{1,0:T(8,128)} %mode_x.1) | copy-start | bytes 18436
  0.7 1.3 %copy-start.3 = (f32[12,32]{1,0:T(8,128)S(1)}, f32[12,32]{1,0:T(8,128)}, u32[]{:S(2)}) copy-start(f32[12,32]{1,0:T(8,128)} %mode_z.1) | copy-start | bytes 4612
  0.7 1.3 %copy-start.4 = (s32[4,12]{1,0:T(4,128)S(1)}, s32[4,12]{1,0:T(4,128)}, u32[]{:S(2)}) copy-start(s32[4,12]{1,0:T(4,128)} %node_c.1) | copy-start | bytes 580
  0.7 1.3 %copy-start.5 = (s32[1,12]{1,0:T(1,128)S(1)}, s32[1,12]{1,0:T(1,128)}, u32[]{:S(2)}) copy-start(s32[1,12]{1,0:T(1,128)} %node_f.1) | copy-start | bytes 148
  0.7 1.3 %copy-start.6 = (s32[4]{0:T(128)S(1)}, s32[4]{0:T(128)}, u32[]{:S(2)}) copy-start(s32[4]{0:T(128)} %w_c.1) | copy-start | bytes 52
  2.0 1.2 %copy-start = (f32[16,32,512]{2,1,0:T(8,128)S(1)}, f32[16,32,512]{2,1,0:T(8,128)}, u32[]{:S(2)}) copy-start(f32[16,32,512]{2,1,0:T(8,128)} %src_f.1) | copy-start | bytes 3145732

commit v2 on v1

v2 whole, which is shorter than its diff:
```python
import math

import jax
import jax.numpy as jnp
import numpy as np
from jax import lax
from jax.experimental import pallas as pl
from jax.experimental.pallas import tpu as pltpu
from jax.sharding import PartitionSpec as P

NODES = 9
SWEEPS = 3
CENTRE = 1.125
HALF_WIDTH = 0.875
SPREAD_RATIO = CENTRE / HALF_WIDTH
LOG2E = 1.0 / math.log(2.0)

F32 = jnp.float32
BF16 = jnp.bfloat16
MESH = pl.DeviceIdType.MESH

TILES = 8
MEMBERS = 16
KL = 12
KP = 16
XS = 16
XC = 8
XPAD = 8
OUTSIDE = -1024.0


def sweep_factors(sweep_count):
    previous = 1.0 / SPREAD_RATIO
    factors = []
    for _ in range(sweep_count - 1):
        current = 1.0 / (2.0 * SPREAD_RATIO - previous)
        factors.append((current * previous, 2.0 * current / HALF_WIDTH))
        previous = current
    return factors


(KEEP1, PUSH1), (KEEP2, PUSH2) = sweep_factors(SWEEPS)
FIRST = 1.0 / CENTRE
SHARE = (1.0 - FIRST) / FIRST
SECOND = PUSH1 * FIRST
BETA = KEEP1 / PUSH1 + SHARE
LEFT = (1.0 - PUSH1) * FIRST
A1 = FIRST + PUSH2 * (LEFT * (SHARE - BETA) - KEEP1 * FIRST)
A2 = (1.0 + KEEP2) * SECOND + PUSH2 * LEFT
A3 = PUSH2 * SECOND
R1 = A1 / A3
R2 = A2 / A3


def iota(shape, dim):
    return lax.broadcasted_iota(jnp.int32, shape, dim)


def halves(value):
    high = value.astype(BF16)
    return high, (value - high.astype(F32)).astype(BF16)


def thirds(value):
    high = value.astype(BF16)
    rest = value - high.astype(F32)
    middle = rest.astype(BF16)
    return high, middle, (rest - middle.astype(F32)).astype(BF16)


def cut(value, low, high, axis):
    return lax.slice_in_dim(value, low, high, axis=axis)


def faces(c, axis, roll_axis, size, first, last):
    n = c.shape[axis]
    head, tail = cut(c, 0, 1, axis), cut(c, n - 1, n, axis)
    wrap = tail + jnp.where(last, 0.0, pltpu.roll(head, size - 1, roll_axis))
    closed = jnp.where(last, 0.0, wrap)
    inner = cut(c, 0, n - 1, axis) + cut(c, 1, n, axis)
    down = jnp.where(first, head, pltpu.roll(closed, 1, roll_axis))
    up = jnp.concatenate([inner, wrap], axis)
    return jnp.concatenate([inner, closed], axis), up + jnp.concatenate([down, inner], axis)


def along(face, v, axis, roll_axis, size):
    n = v.shape[axis]
    inner, wrap = cut(face, 0, n - 1, axis), cut(face, n - 1, n, axis)
    up = jnp.concatenate(
        [inner * cut(v, 1, n, axis), wrap * pltpu.roll(cut(v, 0, 1, axis), size - 1, roll_axis)], axis
    )
    down = jnp.concatenate(
        [pltpu.roll(wrap * cut(v, n - 1, n, axis), 1, roll_axis), inner * cut(v, 0, n - 1, axis)], axis
    )
    return up + down


def pull(fx_low, fx_high, fy, fz, low, here, high):
    d = here.ndim
    across = fx_low * low + fx_high * high
    return (across + along(fy, here, d - 4, d - 1, 128)) + along(fz, here, d - 3, d - 2, 8)


def node_column(node_row):
    value = jnp.zeros(node_row.shape, F32)
    for node in range(NODES):
        value = jnp.where(
            node_row == node, math.cos(math.pi * node / (NODES - 1)) * LOG2E, value
        )
    spread = jnp.broadcast_to(value, (KP, KL))
    own = iota((KP, KL), 0) == iota((KP, KL), 1)
    return jnp.sum(jnp.where(own, spread, 0.0), axis=1, keepdims=True)


def block_transpose(blocks, width, lanes):
    count = len(blocks)
    place = lanes // width
    blocks = list(blocks)
    bit = 1
    while bit < count:
        clear = (place & bit) == 0
        for low in range(count):
            if low & bit:
                continue
            a, b = blocks[low], blocks[low | bit]
            blocks[low] = jnp.where(clear, a, pltpu.roll(b, width * bit, 1))
            blocks[low | bit] = jnp.where(clear, pltpu.roll(a, 128 - width * bit, 1), b)
        bit *= 2
    return blocks


def kernel(
    node_f,
    node_c,
    w_f,
    w_c,
    mode_x,
    mode_y,
    mode_z,
    src_f,
    src_c,
    perm_wide,
    perm_small,
    out,
    fraw,
    craw,
    cpack,
    cgot,
    nodes_f,
    nodes_c,
    weight_f,
    weight_c,
    mx,
    my_in,
    mz,
    mpad,
    xt,
    zt,
    perm_f,
    perm_c,
    rhs_f,
    rhs_c,
    c_f,
    c_c,
    inv_f,
    g_f,
    e_f,
    fx_f,
    fy_f,
    fz_f,
    fcoarse,
    inv_c,
    g_c,
    e_c,
    fx_c,
    fy_c,
    fz_c,
    tot,
    sendbuf,
    recvbuf,
    sumbuf,
    lastbuf,
    local_sem,
    halo_send,
    halo_recv,
    cs_send,
    cs_recv,
    fin_send,
    fin_recv,
    last_send,
    last_recv,
):
    me_m = lax.axis_index("member")
    me_t = lax.axis_index("tile")

    def to(member, tile):
        return {"member": member, "tile": tile}

    def bring(index, source, target):
        copy = pltpu.make_async_copy(source, target, local_sem.at[index])
        copy.start()
        return copy

    own_c = bring(0, src_c, craw)
    small = [
        bring(1, node_f, nodes_f),
        bring(2, node_c, nodes_c),
        bring(3, w_f, weight_f),
        bring(4, w_c, weight_c),
        bring(5, mode_x, mx),
        bring(6, mode_y, my_in),
        bring(7, mode_z, mz),
    ]
    perm = [bring(8, perm_wide, perm_f), bring(9, perm_small, perm_c)]
    own_f = [
        bring(10 + q, src_f.at[:, :, pl.ds(128 * q, 128)], fraw.at[pl.ds(2, XS), q])
        for q in range(4)
    ]

    barrier = pltpu.get_barrier_semaphore()
    for step in range(1, TILES):
        pl.semaphore_signal(
            barrier,
            inc=1,
            device_id=to(me_m, lax.rem(me_t + step, TILES)),
            device_id_type=MESH,
        )
    for step in range(1, MEMBERS):
        pl.semaphore_signal(
            barrier,
            inc=1,
            device_id=to(lax.rem(me_m + step, MEMBERS), me_t),
            device_id_type=MESH,
        )
    partner = to(2 * me_t + lax.rem(me_m, 2), me_m // 2)
    owns = me_m // 2 == me_t

    @pl.when(jnp.logical_not(owns))
    def _():
        pl.semaphore_signal(barrier, inc=1, device_id=partner, device_id_type=MESH)

    lanes = iota((8, 128), 1)
    subs = iota((8, 128), 0)
    masks = (lanes == 0, lanes == 127, subs == 0, subs == 7)

    own_c.wait()
    cpack[0:8] = jnp.zeros((8, 128), F32)
    cpack[264:272] = jnp.zeros((8, 128), F32)
    for quarter in range(4):
        rows = craw[4 * quarter : 4 * quarter + 4].reshape(128, 64)
        cpack[pl.ds(8 + quarter, 64, stride=4), :] = rows.T

    def interleave(parts):
        blocks = []
        for v in range(2):
            low = parts[0][:, 128 * v : 128 * v + 128]
            high = parts[1][:, 128 * v : 128 * v + 128]
            near = iota(low.shape, 1) < 64
            blocks.append(jnp.where(near, low, high))
            blocks.append(pltpu.roll(jnp.where(near, high, low), 64, 1))
        return jnp.concatenate(blocks, 1)

    for copy in small:
        copy.wait()
    for copy in perm:
        copy.wait()
    mpad[...] = jnp.zeros(mpad.shape, F32)
    mpad[0:KL, :] = my_in[...]
    parts = jnp.concatenate(thirds(mpad[...]), 0)
    my = 0.5 * interleave(
        [
            jnp.dot(
                parts[:, 256 * h : 256 * h + 256],
                perm_f[256 * h : 256 * h + 256, :],
                preferred_element_type=F32,
            )
            for h in range(2)
        ]
    )
    my = (my[0:KP] + my[KP : 2 * KP]) + my[2 * KP : 3 * KP]
    mpad[0:KL, 0:128] = mx[...]
    stacked = jnp.concatenate([mpad[:, 0:128]] * 8, 0)
    spare = jnp.where(iota((XPAD, 128), 1) == KL, 1.0, 0.0)
    xt[0:XPAD, :] = spare
    xt[XPAD : XPAD + 128, :] = stacked.T
    xt[XPAD + 128 : XPAD + 128 + XPAD, :] = spare
    mpad[0:KL, 0:32] = mz[...]
    stacked = jnp.concatenate([mpad[:, 0:32]] * 8, 0)
    zt[...] = jnp.where(iota((32, 128), 1) == KL, 1.0, stacked.T)
    zf = [zt[pl.ds(j, 8, stride=4), :] for j in range(4)]
    zc = [0.5 * (zf[2 * j] + zf[2 * j + 1]) for j in range(2)]
    zf = jnp.concatenate(zf, 0)
    zc = jnp.concatenate(zc, 0)

    def sides(value):
        high, low = halves(jnp.where(iota(value.shape, 0) == KL, OUTSIDE, value))
        return jnp.concatenate([high, low, high, low], 0)

    rhs_f[64:128, :] = jnp.zeros((64, 512), BF16)
    rhs_c[64:128, :] = jnp.zeros((64, 1024), BF16)
    rhs_f[0:64, :] = sides(my * node_column(nodes_f[...]))
    myc = jnp.concatenate(
        [
            0.5 * (my[:, 256 * k : 256 * k + 128] + my[:, 256 * k + 128 : 256 * k + 256])
            for k in range(2)
        ],
        1,
    )
    for m in range(4):
        rhs_c[0:64, 256 * m : 256 * m + 256] = sides(myc * node_column(nodes_c[m : m + 1, :]))

    def left(value):
        high = value.astype(BF16).astype(F32)
        return jnp.where(iota(value.shape, 1) < 32, high, value - high).astype(BF16)

    x0 = me_t * XS

    rows = []
    for i in range(XS + 6):
        rows.append(left(xt[pl.ds(x0 - 3 + XPAD + i, 1), :] * zf))
    logs = jnp.dot(jnp.concatenate(rows, 0), rhs_f[...], preferred_element_type=F32)
    for i in range(XS + 6):
        for k in range(4):
            for j in range(4):
                at = 32 * i + 8 * j
                c_f[i, k, j] = jnp.exp2(logs[at : at + 8, 128 * k : 128 * k + 128])

    pl.semaphore_wait(barrier, 23 - owns.astype(jnp.int32))

    has_left = me_t > 0
    has_right = me_t < TILES - 1

    def halo_copy(q, rightwards):
        if rightwards:
            return pltpu.make_async_remote_copy(
                src_ref=src_f.at[pl.ds(XS - 2, 2), :, pl.ds(128 * q, 128)],
                dst_ref=fraw.at[pl.ds(0, 2), q],
                send_sem=halo_send.at[q],
                recv_sem=halo_recv.at[q],
                device_id=to(me_m, lax.rem(me_t + 1, TILES)),
                device_id_type=MESH,
            )
        return pltpu.make_async_remote_copy(
            src_ref=src_f.at[pl.ds(0, 2), :, pl.ds(128 * q, 128)],
            dst_ref=fraw.at[pl.ds(XS + 2, 2), q],
            send_sem=halo_send.at[4 + q],
            recv_sem=halo_recv.at[4 + q],
            device_id=to(me_m, lax.rem(me_t + TILES - 1, TILES)),
            device_id_type=MESH,
        )

    @pl.when(has_right)
    def _():
        for q in range(4):
            halo_copy(q, True).start()

    @pl.when(has_left)
    def _():
        for q in range(4):
            halo_copy(q, False).start()

    @pl.when(jnp.logical_not(has_left))
    def _():
        fraw[0:2] = jnp.zeros((2, 4, 32, 128), F32)

    @pl.when(jnp.logical_not(has_right))
    def _():
        fraw[XS + 2 : XS + 4] = jnp.zeros((2, 4, 32, 128), F32)

    def strip_rows(tile):
        return cpack.at[pl.ds(pl.multiple_of(32 * tile, 8), 48)]

    def strip_copy(step):
        there = lax.rem(me_t + step, TILES)
        return pltpu.make_async_remote_copy(
            src_ref=strip_rows(there),
            dst_ref=cgot.at[me_t],
            send_sem=cs_send.at[step],
            recv_sem=cs_recv.at[step],
            device_id=to(me_m, there),
            device_id_type=MESH,
        )

    def set_up(planes, c, fx, fy, fz, inv):
        fx[0] = c[0] + c[1]

        def plane(n, carry):
            here = c[n + 1]
            d = here.ndim
            upper = here + c[n + 2]
            y_face, y_sum = faces(here, d - 4, d - 1, 128, masks[0], masks[1])
            z_face, z_sum = faces(here, d - 3, d - 2, 8, masks[2], masks[3])
            total = ((fx[n] + upper) + y_sum) + z_sum
            turned = pltpu.reciprocal(total, approx=True)
            turned = turned * (2.0 - total * turned)
            fx[n + 1] = upper
            fy[n] = y_face
            fz[n] = z_face
            inv[n] = turned
            return carry

        lax.fori_loop(0, planes, plane, 0)

        @pl.when(jnp.logical_not(has_left))
        def _():
            inv[0:2] = jnp.zeros((2,) + inv.shape[1:], F32)

        @pl.when(jnp.logical_not(has_right))
        def _():
            inv[planes - 2 : planes] = jnp.zeros((2,) + inv.shape[1:], F32)

    set_up(XS + 4, c_f, fx_f, fy_f, fz_f, inv_f)

    for step in range(1, TILES):
        strip_copy(step).start()
    cgot[me_t] = strip_rows(me_t)[...]

    rows = []
    for i in range(XC + 6):
        at = x0 - 6 + XPAD + 2 * i
        mean = 0.5 * (xt[pl.ds(at, 1), :] + xt[pl.ds(at + 1, 1), :])
        rows.append(left(mean * zc))
    logs = jnp.dot(jnp.concatenate(rows, 0), rhs_c[...], preferred_element_type=F32)
    for i in range(XC + 6):
        for m in range(4):
            for k in range(2):
                for j in range(2):
                    at, of = 16 * i + 8 * j, 256 * m + 128 * k
                    c_c[i, m, k, j] = jnp.exp2(logs[at : at + 8, of : of + 128])
    set_up(XC + 4, c_c, fx_c, fy_c, fz_c, inv_c)

    for copy in own_f:
        copy.wait()

    @pl.when(has_left)
    def _():
        for q in range(4):
            halo_copy(q, True).wait_recv()

    @pl.when(has_right)
    def _():
        for q in range(4):
            halo_copy(q, False).wait_recv()

    SOURCE_CHUNK = 10

    def source_fine(chunk, carry):
        halves_of_y = []
        for h in range(2):
            rows = []
            for i in range(SOURCE_CHUNK):
                for j in range(4):
                    rows.append(
                        jnp.concatenate(
                            [
                                fraw[SOURCE_CHUNK * chunk + i, 2 * h + q, pl.ds(j, 8, stride=4), :]
                                for q in range(2)
                            ],
                            1,
                        )
                    )
            high, low = halves(jnp.concatenate(rows, 0))
            order = perm_f[256 * h : 256 * h + 256, :]
            halves_of_y.append(
                jnp.dot(high, order, preferred_element_type=F32)
                + jnp.dot(low, order, preferred_element_type=F32)
            )
        got = interleave(halves_of_y)
        for i in range(SOURCE_CHUNK):
            n = SOURCE_CHUNK * chunk + i
            for k in range(4):
                for j in range(4):
                    at = 32 * i + 8 * j
                    g_f[n, k, j] = got[at : at + 8, 128 * k : 128 * k + 128] * inv_f[n, k, j]
        return carry

    lax.fori_loop(0, (XS + 4) // SOURCE_CHUNK, source_fine, 0)

    def sweep(planes, fx, fy, fz, inv, g, e):
        def plane(n, carry):
            here = g[n + 1]
            moved = pull(fx[n + 1], fx[n + 2], fy[n + 1], fz[n + 1], g[n], here, g[n + 2])
            e[n] = BETA * here + moved * inv[n + 1]
            return carry

        lax.fori_loop(0, planes, plane, 0)

    sweep(XS + 2, fx_f, fy_f, fz_f, inv_f, g_f, e_f)

    for step in range(1, TILES):
        strip_copy(step).wait_recv()
    rows = []
    for pair in range(6):
        at = slice(8 * pair, 8 * pair + 8)
        parts = [
            block_transpose([cgot[4 * half + q, at] for q in range(4)], 32, lanes)
            for half in range(2)
        ]
        for r in range(4):
            rows.append(jnp.concatenate([parts[0][r], parts[1][r]], 1))
    high, low = halves(jnp.concatenate(rows, 0))
    got = jnp.dot(high, perm_c[0:256, :], preferred_element_type=F32)
    got = got + jnp.dot(low, perm_c[0:256, :], preferred_element_type=F32)
    for pair in range(6):
        for r in range(4):
            for a in range(2):
                for k in range(2):
                    at = 32 * pair + 8 * r + 4 * a
                    fcoarse[2 * pair + a, k, r % 2, pl.ds(r // 2, 4, stride=2), :] = got[
                        at : at + 4, 128 * k : 128 * k + 128
                    ]
    for n in range(XC + 4):
        g_c[n] = fcoarse[n][None] * inv_c[n]
    sweep(XC + 2, fx_c, fy_c, fz_c, inv_c, g_c, e_c)

    scale_f = jnp.broadcast_to(weight_f[...].astype(F32) * (0.125 * A3), (8, 128))
    scale_c = [
        jnp.broadcast_to(weight_c[:, m : m + 1].astype(F32) * A3, (8, 128)) for m in range(4)
    ]

    def third(n, fx, fy, fz, inv, e):
        moved = pull(fx[n + 2], fx[n + 3], fy[n + 2], fz[n + 2], e[n], e[n + 1], e[n + 2])
        return moved * inv[n + 2]

    def block_sum(pair):
        rows = pair
        out_blocks = []
        for k in range(2):
            for j in range(2):
                out_blocks.append(
                    (rows[2 * k, 2 * j] + rows[2 * k + 1, 2 * j])
                    + (rows[2 * k, 2 * j + 1] + rows[2 * k + 1, 2 * j + 1])
                )
        return out_blocks

    def finish_plane(xc, carry):
        n = 2 * xc
        t_sum = block_sum(
            third(n, fx_f, fy_f, fz_f, inv_f, e_f) + third(n + 1, fx_f, fy_f, fz_f, inv_f, e_f)
        )
        g_sum = block_sum(g_f[n + 2] + g_f[n + 3])
        e_sum = block_sum(e_f[n + 1] + e_f[n + 2])
        coarse = (R1 * g_c[xc + 2] + R2 * e_c[xc + 1]) + third(
            xc, fx_c, fy_c, fz_c, inv_c, e_c
        )
        for k in range(2):
            for j in range(2):
                b = 2 * k + j
                block = scale_f * ((R1 * g_sum[b] + R2 * e_sum[b]) + t_sum[b])
                for m in range(4):
                    block = block + scale_c[m] * coarse[m, k, j]
                tot[xc, k, j] = block
        return carry

    def piece_copy(e, step):
        there = lax.rem(me_m // 2 + step, TILES)
        return pltpu.make_async_remote_copy(
            src_ref=sendbuf.at[e, there],
            dst_ref=recvbuf.at[lax.rem(me_m - 2 * there - e + 2 * MEMBERS, MEMBERS) - 1],
            send_sem=fin_send,
            recv_sem=fin_recv,
            device_id=to(2 * there + e, me_t),
            device_id_type=MESH,
        )

    for e in range(2):
        lax.fori_loop(4 * e, 4 * e + 4, finish_plane, 0)
        for chi in range(2):
            pieces = block_transpose(
                [
                    tot[4 * e + 2 * chi + a, k, j]
                    for a in range(2)
                    for j in range(2)
                    for k in range(2)
                ],
                16,
                lanes,
            )
            for t in range(TILES):
                sendbuf[e, t, 8 * chi : 8 * chi + 8, :] = pieces[t]
        for step in range(1, TILES):
            piece_copy(e, step).start()

        @pl.when(lax.rem(me_m, 2) != e)
        def _():
            piece_copy(e, 0).start()

    @pl.when(has_right)
    def _():
        for q in range(4):
            halo_copy(q, True).wait_send()

    @pl.when(has_left)
    def _():
        for q in range(4):
            halo_copy(q, False).wait_send()

    for step in range(1, TILES):
        strip_copy(step).wait_send()

    arrivals = pltpu.make_async_remote_copy(
        src_ref=recvbuf,
        dst_ref=recvbuf,
        send_sem=fin_send,
        recv_sem=fin_recv,
        device_id=to(lax.rem(me_m + 1, MEMBERS), me_t),
        device_id_type=MESH,
    )
    arrivals.wait_recv()
    terms = [sendbuf[lax.rem(me_m, 2), me_m // 2]] + [recvbuf[i] for i in range(MEMBERS - 1)]
    while len(terms) > 1:
        terms = [a + b for a, b in zip(terms[0::2], terms[1::2])]
    order = perm_c[256:384, 0:128]
    flat = sum(jnp.dot(part, order, preferred_element_type=F32) for part in thirds(terms[0]))
    last = pltpu.make_async_remote_copy(
        src_ref=sumbuf,
        dst_ref=lastbuf,
        send_sem=last_send,
        recv_sem=last_recv,
        device_id=partner,
        device_id_type=MESH,
    )
    sumbuf[...] = flat

    @pl.when(owns)
    def _():
        lastbuf[...] = sumbuf[...]

    @pl.when(jnp.logical_not(owns))
    def _():
        last.start()
        last.wait_recv()

    for chi in range(2):
        for g in range(4):
            out[2 * chi + g // 2, pl.ds(g % 2, 8, stride=2), :] = lastbuf[
                8 * chi : 8 * chi + 8, 32 * g : 32 * g + 32
            ]

    arrivals.wait_send()

    @pl.when(jnp.logical_not(owns))
    def _():
        last.wait_send()


def permutations():
    col = np.arange(256)
    wide = np.zeros((512, 256), np.float32)
    k = 2 * (col // 128) + (col % 128) // 64
    wide[4 * (col % 64) + k, col] = 2.0
    k = 2 * (col // 128) + 1 - (col % 128) // 64
    wide[256 + 4 * (col % 64) + k, col] = 2.0
    col = np.arange(256)
    small = np.zeros((384, 256), np.float32)
    small[2 * (col % 128) + col // 128, col] = 2.0
    row = np.arange(128)
    small[256 + row, (row & 96) + 2 * (row & 15) + ((row >> 4) & 1)] = 1.0
    return jnp.asarray(wide, BF16), jnp.asarray(small, BF16)


def body(
    node_fine,
    node_coarse,
    weight_fine,
    weight_coarse,
    mode_x,
    mode_y,
    mode_z,
    source_fine,
    source_coarse,
):
    hbm = pl.BlockSpec(memory_space=pl.ANY)
    fine = (4, 4, 8, 128)
    flat = (2, 2, 8, 128)
    coarse = (4, 2, 2, 8, 128)
    dma = pltpu.SemaphoreType.DMA

    def vmem(*shape, dtype=F32):
        return pltpu.VMEM(shape, dtype)

    scratch = [
        vmem(XS + 4, 4, 32, 128),
        vmem(16, 32, 64),
        vmem(272, 128),
        vmem(TILES, 48, 128),
        vmem(1, KL, dtype=jnp.int32),
        vmem(4, KL, dtype=jnp.int32),
        vmem(1, 1, dtype=jnp.int32),
        vmem(1, 4, dtype=jnp.int32),
        vmem(KL, 128),
        vmem(KL, 512),
        vmem(KL, 32),
        vmem(KP, 512),
        vmem(XPAD + 128 + XPAD, 128),
        vmem(32, 128),
        vmem(512, 256, dtype=BF16),
        vmem(384, 256, dtype=BF16),
        vmem(128, 512, dtype=BF16),
        vmem(128, 1024, dtype=BF16),
        vmem(XS + 6, *fine),
        vmem(XC + 6, *coarse),
        vmem(XS + 4, *fine),
        vmem(XS + 4, *fine),
        vmem(XS + 2, *fine),
        vmem(XS + 5, *fine),
        vmem(XS + 4, *fine),
        vmem(XS + 4, *fine),
        vmem(XC + 4, *flat),
        vmem(XC + 4, *coarse),
        vmem(XC + 4, *coarse),
        vmem(XC + 2, *coarse),
        vmem(XC + 5, *coarse),
        vmem(XC + 4, *coarse),
        vmem(XC + 4, *coarse),
        vmem(XC, *flat),
        vmem(2, TILES, 16, 128),
        vmem(MEMBERS - 1, 16, 128),
        vmem(16, 128),
        vmem(16, 128),
        dma((14,)),
        dma((8,)),
        dma((8,)),
        dma((TILES,)),
        dma((TILES,)),
        dma(()),
        dma(()),
        dma(()),
        dma(()),
    ]
    return pl.pallas_call(
        kernel,
        out_shape=jax.ShapeDtypeStruct((4, 16, 32), F32),
        in_specs=[hbm] * 11,
        out_specs=pl.BlockSpec(memory_space=pltpu.VMEM),
        scratch_shapes=scratch,
        compiler_params=pltpu.CompilerParams(
            collective_id=0, has_side_effects=True, vmem_limit_bytes=60 * 2**20
        ),
    )(
        node_fine,
        node_coarse,
        weight_fine.reshape(1, 1),
        weight_coarse.reshape(1, 4),
        mode_x,
        mode_y,
        mode_z,
        source_fine,
        jnp.transpose(source_coarse, (1, 2, 0)),
        *permutations(),
    )


def solution(mesh):
    return jax.shard_map(
        body,
        mesh=mesh,
        in_specs=(
            P("member", None),
            P("member", None),
            P("member"),
            P("member"),
            P(),
            P(),
            P(),
            P("tile", None, None),
            P(None, None, "tile"),
        ),
        out_specs=P("member", None, "tile"),
        check_vma=False,
    )
```

time: 34.3 us -> 30.5 us (0.89)
  the two profiles are of different devices: /device:TPU:37 before, /device:TPU:39 now
where the time goes in v2:
time: 30.5 us; the launch traced here: 30.3 us
  Pallas kernels  28.2 us (92%)
  local copies, waits for them, and re-layouts  1.38 us (5%)
  between operations  0.66 us (2%)
    pallas_call x1, Pallas kernels, body(): pl.pallas_call(kernel, out_shape=jax.ShapeDtypeStruct((4, 16, 32), F32),...  28.2 us
    unnamed x1, local copies, waits for them, and re-layouts  1.38 us

profile of v2, /device:TPU:39, one launch (start us, length us, event | category | flops | bytes accessed | tf_op | source)
XLA Modules:
  0.0 30.3 jit_solution(3554680663292220949)
XLA Ops:
  0.7 28.2 %shard_map.109 = f32[4,16,32]{2,1,0:T(8,128)} custom-call(s32[1,12]{1,0:T(1,128)} %node_f.1, s32[4,12]{1,0:T(4,128)} %node_c.1, s32[1,1]{1,0:T(1,128)} %bitcast.3.w_f, s32[1,4]{1,0:T(1,128)} %bitcast.5, f32[12,128]{1,0:T(8,128)} %mode_x.1, f32[12,512]{1,0:T(8,128)} %mode_y.1, f32[12,32]{1,0:T(8,128)} %mode_z.1, f32[16,32,512]{2,1,0:T(8,128)} %src_f.1, ...), custom_call_target="tpu_custom_call" | custom-call | tf_op jit(solution)/shard_map/pallas_call | solution.py:731
  28.9 1.4 %copy.14 = f32[4,16,32]{2,1,0:T(8,128)} copy(f32[4,16,32]{2,1,0:T(8,128)} %shard_map.109) | data formatting | bytes 16384

commit v3 on v2

--- a/solution.py
+++ b/solution.py
@@ -177,18 +177,18 @@
     fz_c,
     tot,
     sendbuf,
+    sharebuf,
+    outbuf,
     recvbuf,
-    sumbuf,
-    lastbuf,
     local_sem,
     halo_send,
     halo_recv,
     cs_send,
     cs_recv,
+    fwd_send,
+    fwd_recv,
     fin_send,
     fin_recv,
-    last_send,
-    last_recv,
 ):
     me_m = lax.axis_index("member")
     me_t = lax.axis_index("tile")
@@ -201,7 +201,6 @@
         copy.start()
         return copy
 
-    own_c = bring(0, src_c, craw)
     small = [
         bring(1, node_f, nodes_f),
         bring(2, node_c, nodes_c),
@@ -211,6 +210,7 @@
         bring(6, mode_y, my_in),
         bring(7, mode_z, mz),
     ]
+    own_c = bring(0, src_c, craw)
     perm = [bring(8, perm_wide, perm_f), bring(9, perm_small, perm_c)]
     own_f = [
         bring(10 + q, src_f.at[:, :, pl.ds(128 * q, 128)], fraw.at[pl.ds(2, XS), q])
@@ -225,19 +225,18 @@
             device_id=to(me_m, lax.rem(me_t + step, TILES)),
             device_id_type=MESH,
         )
-    for step in range(1, MEMBERS):
+    core = lax.rem(me_m, 2)
+    sibling = to(me_m + 1 - 2 * core, me_t)
+    pl.semaphore_signal(barrier, inc=1, device_id=sibling, device_id_type=MESH)
+    feeding_tile = me_m // 2
+    for step in range(2, MEMBERS, 2):
         pl.semaphore_signal(
             barrier,
             inc=1,
-            device_id=to(lax.rem(me_m + step, MEMBERS), me_t),
+            device_id=to(lax.rem(me_m + step, MEMBERS), feeding_tile),
             device_id_type=MESH,
         )
-    partner = to(2 * me_t + lax.rem(me_m, 2), me_m // 2)
-    owns = me_m // 2 == me_t
-
-    @pl.when(jnp.logical_not(owns))
-    def _():
-        pl.semaphore_signal(barrier, inc=1, device_id=partner, device_id_type=MESH)
+    feeds_itself = feeding_tile == me_t
 
     lanes = iota((8, 128), 1)
     subs = iota((8, 128), 0)
@@ -249,6 +248,66 @@
     for quarter in range(4):
         rows = craw[4 * quarter : 4 * quarter + 4].reshape(128, 64)
         cpack[pl.ds(8 + quarter, 64, stride=4), :] = rows.T
+
+    pl.semaphore_wait(barrier, 16 - 8 * feeds_itself.astype(jnp.int32))
+
+    has_left = me_t > 0
+    has_right = me_t < TILES - 1
+
+    def halo_copy(q, rightwards):
+        here = pl.ds(pl.multiple_of(256 * core + 128 * q, 128), 128)
+        if rightwards:
+            return pltpu.make_async_remote_copy(
+                src_ref=src_f.at[pl.ds(XS - 2, 2), :, here],
+                dst_ref=fraw.at[pl.ds(0, 2), 2 * core + q],
+                send_sem=halo_send.at[q],
+                recv_sem=halo_recv.at[q],
+                device_id=to(me_m, lax.rem(me_t + 1, TILES)),
+                device_id_type=MESH,
+            )
+        return pltpu.make_async_remote_copy(
+            src_ref=src_f.at[pl.ds(0, 2), :, here],
+            dst_ref=fraw.at[pl.ds(XS + 2, 2), 2 * core + q],
+            send_sem=halo_send.at[2 + q],
+            recv_sem=halo_recv.at[2 + q],
+            device_id=to(me_m, lax.rem(me_t + TILES - 1, TILES)),
+            device_id_type=MESH,
+        )
+
+    def hand_over(index, part):
+        return pltpu.make_async_remote_copy(
+            src_ref=part,
+            dst_ref=part,
+            send_sem=fwd_send.at[index],
+            recv_sem=fwd_recv.at[index],
+            device_id=sibling,
+            device_id_type=MESH,
+        )
+
+    halo_over = [
+        hand_over(0, fraw.at[pl.ds(0, 2), pl.ds(2 * core, 2)]),
+        hand_over(1, fraw.at[pl.ds(XS + 2, 2), pl.ds(2 * core, 2)]),
+    ]
+    own_rows = pl.ds(pl.multiple_of(24 * core, 8), 24)
+    strip_over = hand_over(2, cgot.at[:, own_rows])
+
+    @pl.when(has_right)
+    def _():
+        for q in range(2):
+            halo_copy(q, True).start()
+
+    @pl.when(has_left)
+    def _():
+        for q in range(2):
+            halo_copy(q, False).start()
+
+    @pl.when(jnp.logical_not(has_left))
+    def _():
+        fraw[0:2] = jnp.zeros((2, 4, 32, 128), F32)
+
+    @pl.when(jnp.logical_not(has_right))
+    def _():
+        fraw[XS + 2 : XS + 4] = jnp.zeros((2, 4, 32, 128), F32)
 
     def interleave(parts):
         blocks = []
@@ -325,61 +384,23 @@
                 at = 32 * i + 8 * j
                 c_f[i, k, j] = jnp.exp2(logs[at : at + 8, 128 * k : 128 * k + 128])
 
-    pl.semaphore_wait(barrier, 23 - owns.astype(jnp.int32))
-
-    has_left = me_t > 0
-    has_right = me_t < TILES - 1
-
-    def halo_copy(q, rightwards):
-        if rightwards:
-            return pltpu.make_async_remote_copy(
-                src_ref=src_f.at[pl.ds(XS - 2, 2), :, pl.ds(128 * q, 128)],
-                dst_ref=fraw.at[pl.ds(0, 2), q],
-                send_sem=halo_send.at[q],
-                recv_sem=halo_recv.at[q],
-                device_id=to(me_m, lax.rem(me_t + 1, TILES)),
-                device_id_type=MESH,
-            )
-        return pltpu.make_async_remote_copy(
-            src_ref=src_f.at[pl.ds(0, 2), :, pl.ds(128 * q, 128)],
-            dst_ref=fraw.at[pl.ds(XS + 2, 2), q],
-            send_sem=halo_send.at[4 + q],
-            recv_sem=halo_recv.at[4 + q],
-            device_id=to(me_m, lax.rem(me_t + TILES - 1, TILES)),
-            device_id_type=MESH,
-        )
-
-    @pl.when(has_right)
-    def _():
-        for q in range(4):
-            halo_copy(q, True).start()
-
-    @pl.when(has_left)
-    def _():
-        for q in range(4):
-            halo_copy(q, False).start()
-
-    @pl.when(jnp.logical_not(has_left))
-    def _():
-        fraw[0:2] = jnp.zeros((2, 4, 32, 128), F32)
-
-    @pl.when(jnp.logical_not(has_right))
-    def _():
-        fraw[XS + 2 : XS + 4] = jnp.zeros((2, 4, 32, 128), F32)
-
     def strip_rows(tile):
-        return cpack.at[pl.ds(pl.multiple_of(32 * tile, 8), 48)]
+        return cpack.at[pl.ds(pl.multiple_of(32 * tile + 24 * core, 8), 24)]
 
     def strip_copy(step):
         there = lax.rem(me_t + step, TILES)
         return pltpu.make_async_remote_copy(
             src_ref=strip_rows(there),
-            dst_ref=cgot.at[me_t],
+            dst_ref=cgot.at[me_t, own_rows],
             send_sem=cs_send.at[step],
             recv_sem=cs_recv.at[step],
             device_id=to(me_m, there),
             device_id_type=MESH,
         )
+
+    for step in range(1, TILES):
+        strip_copy(step).start()
+    cgot[me_t, own_rows] = strip_rows(me_t)[...]
 
     def set_up(planes, c, fx, fy, fz, inv):
         fx[0] = c[0] + c[1]
@@ -392,14 +413,13 @@
             z_face, z_sum = faces(here, d - 3, d - 2, 8, masks[2], masks[3])
             total = ((fx[n] + upper) + y_sum) + z_sum
             turned = pltpu.reciprocal(total, approx=True)
-            turned = turned * (2.0 - total * turned)
             fx[n + 1] = upper
             fy[n] = y_face
             fz[n] = z_face
             inv[n] = turned
             return carry
 
-        lax.fori_loop(0, planes, plane, 0)
+        lax.fori_loop(0, planes, plane, 0, unroll=4 if planes == XS + 4 else 4)
 
         @pl.when(jnp.logical_not(has_left))
         def _():
@@ -411,9 +431,18 @@
 
     set_up(XS + 4, c_f, fx_f, fy_f, fz_f, inv_f)
 
-    for step in range(1, TILES):
-        strip_copy(step).start()
-    cgot[me_t] = strip_rows(me_t)[...]
+    @pl.when(has_left)
+    def _():
+        for q in range(2):
+            halo_copy(q, True).wait_recv()
+        halo_over[0].start()
+
+    @pl.when(has_right)
+    def _():
+        for q in range(2):
+            halo_copy(q, False).wait_recv()
+        halo_over[1].start()
+
 
     rows = []
     for i in range(XC + 6):
@@ -429,18 +458,20 @@
                     c_c[i, m, k, j] = jnp.exp2(logs[at : at + 8, of : of + 128])
     set_up(XC + 4, c_c, fx_c, fy_c, fz_c, inv_c)
 
+    for step in range(1, TILES):
+        strip_copy(step).wait_recv()
+    strip_over.start()
+
     for copy in own_f:
         copy.wait()
 
     @pl.when(has_left)
     def _():
-        for q in range(4):
-            halo_copy(q, True).wait_recv()
+        halo_over[0].wait_recv()
 
     @pl.when(has_right)
     def _():
-        for q in range(4):
-            halo_copy(q, False).wait_recv()
+        halo_over[1].wait_recv()
 
     SOURCE_CHUNK = 10
 
@@ -483,12 +514,11 @@
             e[n] = BETA * here + moved * inv[n + 1]
             return carry
 
-        lax.fori_loop(0, planes, plane, 0)
+        lax.fori_loop(0, planes, plane, 0, unroll=3 if planes == XS + 2 else 5)
 
     sweep(XS + 2, fx_f, fy_f, fz_f, inv_f, g_f, e_f)
 
-    for step in range(1, TILES):
-        strip_copy(step).wait_recv()
+    strip_over.wait_recv()
     rows = []
     for pair in range(6):
         at = slice(8 * pair, 8 * pair + 8)
@@ -552,96 +582,117 @@
                 tot[xc, k, j] = block
         return carry
 
-    def piece_copy(e, step):
-        there = lax.rem(me_m // 2 + step, TILES)
+    def pieces_of(first):
+        return block_transpose(
+            [tot[first + a, k, j] for a in range(2) for j in range(2) for k in range(2)],
+            16,
+            lanes,
+        )
+
+    def finish_planes(first, count):
+        def one(i, carry):
+            return finish_plane(first + i, carry)
+
+        lax.fori_loop(0, count, one, 0, unroll=2)
+
+    other = 1 - core
+    finish_planes(4 * other, 4)
+    for chi in range(2):
+        pieces = pieces_of(4 * other + 2 * chi)
+        for t in range(TILES):
+            sendbuf[chi, t] = pieces[t]
+    share = pltpu.make_async_remote_copy(
+        src_ref=sendbuf,
+        dst_ref=sharebuf,
+        send_sem=fwd_send.at[3],
+        recv_sem=fwd_recv.at[3],
+        device_id=sibling,
+        device_id_type=MESH,
+    )
+    share.start()
+
+    def piece_copy(chi, step):
+        there = lax.rem(me_t + step, TILES)
         return pltpu.make_async_remote_copy(
-            src_ref=sendbuf.at[e, there],
-            dst_ref=recvbuf.at[lax.rem(me_m - 2 * there - e + 2 * MEMBERS, MEMBERS) - 1],
+            src_ref=outbuf.at[chi, there],
+            dst_ref=recvbuf.at[me_m // 2, chi],
             send_sem=fin_send,
             recv_sem=fin_recv,
-            device_id=to(2 * there + e, me_t),
+            device_id=to(2 * me_t + core, there),
             device_id_type=MESH,
         )
 
-    for e in range(2):
-        lax.fori_loop(4 * e, 4 * e + 4, finish_plane, 0)
-        for chi in range(2):
-            pieces = block_transpose(
-                [
-                    tot[4 * e + 2 * chi + a, k, j]
-                    for a in range(2)
-                    for j in range(2)
-                    for k in range(2)
-                ],
-                16,
-                lanes,
-            )
-            for t in range(TILES):
-                sendbuf[e, t, 8 * chi : 8 * chi + 8, :] = pieces[t]
+    for chi in range(2):
+        finish_planes(4 * core + 2 * chi, 2)
+        if chi == 0:
+            share.wait_recv()
+        pieces = pieces_of(4 * core + 2 * chi)
+        for t in range(TILES):
+            outbuf[chi, t] = pieces[t] + sharebuf[chi, t]
         for step in range(1, TILES):
-            piece_copy(e, step).start()
-
-        @pl.when(lax.rem(me_m, 2) != e)
+            piece_copy(chi, step).start()
+
+        @pl.when(feeds_itself)
         def _():
-            piece_copy(e, 0).start()
+            recvbuf[me_m // 2, chi] = outbuf[chi, me_t]
+
+        @pl.when(jnp.logical_not(feeds_itself))
+        def _():
+            piece_copy(chi, 0).start()
 
     @pl.when(has_right)
     def _():
-        for q in range(4):
+        for q in range(2):
             halo_copy(q, True).wait_send()
+        halo_over[1].wait_send()
 
     @pl.when(has_left)
     def _():
-        for q in range(4):
+        for q in range(2):
             halo_copy(q, False).wait_send()
+        halo_over[0].wait_send()
 
     for step in range(1, TILES):
         strip_copy(step).wait_send()
-
-    arrivals = pltpu.make_async_remote_copy(
-        src_ref=recvbuf,
-        dst_ref=recvbuf,
-        send_sem=fin_send,
-        recv_sem=fin_recv,
-        device_id=to(lax.rem(me_m + 1, MEMBERS), me_t),
-        device_id_type=MESH,
-    )
-    arrivals.wait_recv()
-    terms = [sendbuf[lax.rem(me_m, 2), me_m // 2]] + [recvbuf[i] for i in range(MEMBERS - 1)]
+    strip_over.wait_send()
+    share.wait_send()
+
+    def arrivals(count):
+        return pltpu.make_async_remote_copy(
+            src_ref=recvbuf.at[pl.ds(0, count)],
+            dst_ref=recvbuf.at[pl.ds(0, count)],
+            send_sem=fin_send,
+            recv_sem=fin_recv,
+            device_id=to(me_m, lax.rem(me_t + 1, TILES)),
+            device_id_type=MESH,
+        )
+
+    @pl.when(feeds_itself)
+    def _():
+        arrivals(TILES - 1).wait_recv()
+
+    @pl.when(jnp.logical_not(feeds_itself))
+    def _():
+        arrivals(TILES).wait_recv()
+
+    terms = [recvbuf[i].reshape(16, 128) for i in range(TILES)]
     while len(terms) > 1:
         terms = [a + b for a, b in zip(terms[0::2], terms[1::2])]
     order = perm_c[256:384, 0:128]
     flat = sum(jnp.dot(part, order, preferred_element_type=F32) for part in thirds(terms[0]))
-    last = pltpu.make_async_remote_copy(
-        src_ref=sumbuf,
-        dst_ref=lastbuf,
-        send_sem=last_send,
-        recv_sem=last_recv,
-        device_id=partner,
-        device_id_type=MESH,
-    )
-    sumbuf[...] = flat
-
-    @pl.when(owns)
-    def _():
-        lastbuf[...] = sumbuf[...]
-
-    @pl.when(jnp.logical_not(owns))
-    def _():
-        last.start()
-        last.wait_recv()
-
     for chi in range(2):
         for g in range(4):
-            out[2 * chi + g // 2, pl.ds(g % 2, 8, stride=2), :] = lastbuf[
+            out[2 * chi + g // 2, pl.ds(g % 2, 8, stride=2), :] = flat[
                 8 * chi : 8 * chi + 8, 32 * g : 32 * g + 32
             ]
 
-    arrivals.wait_send()
-
-    @pl.when(jnp.logical_not(owns))
-    def _():
-        last.wait_send()
+    @pl.when(feeds_itself)
+    def _():
+        arrivals(TILES - 1).wait_send()
+
+    @pl.when(jnp.logical_not(feeds_itself))
+    def _():
+        arrivals(TILES).wait_send()
 
 
 def permutations():
@@ -714,17 +765,17 @@
         vmem(XC + 4, *coarse),
         vmem(XC + 4, *coarse),
         vmem(XC, *flat),
-        vmem(2, TILES, 16, 128),
-        vmem(MEMBERS - 1, 16, 128),
-        vmem(16, 128),
-        vmem(16, 128),
+        vmem(2, TILES, 8, 128),
+        vmem(2, TILES, 8, 128),
+        vmem(2, TILES, 8, 128),
+        vmem(TILES, 2, 8, 128),
         dma((14,)),
-        dma((8,)),
-        dma((8,)),
+        dma((4,)),
+        dma((4,)),
         dma((TILES,)),
         dma((TILES,)),
-        dma(()),
-        dma(()),
+        dma((4,)),
+        dma((4,)),
         dma(()),
         dma(()),
     ]

time: 30.5 us -> 26.4 us (0.87)
  the two profiles are of different devices: /device:TPU:39 before, /device:TPU:36 now
where the time goes in v3:
time: 26.4 us; the launch traced here: 26.2 us
  Pallas kernels  24.2 us (92%)
  local copies, waits for them, and re-layouts  1.38 us (5%)
  between operations  0.66 us (2%)
    pallas_call x1, Pallas kernels, body(): pl.pallas_call(kernel, out_shape=jax.ShapeDtypeStruct((4, 16, 32), F32),...  24.2 us
    unnamed x1, local copies, waits for them, and re-layouts  1.38 us

profile of v3, /device:TPU:36, one launch (start us, length us, event | category | flops | bytes accessed | tf_op | source)
XLA Modules:
  0.0 26.2 jit_solution(8604749299869567776)
XLA Ops:
  0.7 24.2 %shard_map.109 = f32[4,16,32]{2,1,0:T(8,128)} custom-call(s32[1,12]{1,0:T(1,128)} %node_f.1, s32[4,12]{1,0:T(4,128)} %node_c.1, s32[1,1]{1,0:T(1,128)} %bitcast.3.w_f, s32[1,4]{1,0:T(1,128)} %bitcast.5, f32[12,128]{1,0:T(8,128)} %mode_x.1, f32[12,512]{1,0:T(8,128)} %mode_y.1, f32[12,32]{1,0:T(8,128)} %mode_z.1, f32[16,32,512]{2,1,0:T(8,128)} %src_f.1, ...), custom_call_target="tpu_custom_call" | custom-call | tf_op jit(solution)/shard_map/pallas_call | solution.py:782
  24.8 1.4 %copy.14 = f32[4,16,32]{2,1,0:T(8,128)} copy(f32[4,16,32]{2,1,0:T(8,128)} %shard_map.109) | data formatting | bytes 16384

commit v4 on v0

v4 whole, which is shorter than its diff:
```python
import math

import jax
import jax.numpy as jnp
import numpy as np
from jax import lax
from jax.experimental import pallas as pl
from jax.experimental.pallas import tpu as pltpu
from jax.sharding import PartitionSpec as P

NODES = 9
SWEEPS = 3
CENTRE = 1.125
HALF_WIDTH = 0.875
SPREAD_RATIO = CENTRE / HALF_WIDTH
LOG2E = 1.0 / math.log(2.0)

F32 = jnp.float32
BF16 = jnp.bfloat16
MESH = pl.DeviceIdType.MESH

TILES = 8
MEMBERS = 16
KL = 12
KP = 16
XF = 8
XC = 4
KF = 9
KC = 5
XPAD = 8
OUTSIDE = -1024.0


def sweep_factors(sweep_count):
    previous = 1.0 / SPREAD_RATIO
    factors = []
    for _ in range(sweep_count - 1):
        current = 1.0 / (2.0 * SPREAD_RATIO - previous)
        factors.append((current * previous, 2.0 * current / HALF_WIDTH))
        previous = current
    return factors


(KEEP1, PUSH1), (KEEP2, PUSH2) = sweep_factors(SWEEPS)
FIRST = 1.0 / CENTRE
SHARE = (1.0 - FIRST) / FIRST
SECOND = PUSH1 * FIRST
BETA = KEEP1 / PUSH1 + SHARE
LEFT = (1.0 - PUSH1) * FIRST
A1 = FIRST + PUSH2 * (LEFT * (SHARE - BETA) - KEEP1 * FIRST)
A2 = (1.0 + KEEP2) * SECOND + PUSH2 * LEFT
A3 = PUSH2 * SECOND
R1 = A1 / A3
R2 = A2 / A3


def iota(shape, dim):
    return lax.broadcasted_iota(jnp.int32, shape, dim)


def halves(value):
    high = value.astype(BF16)
    return high, (value - high.astype(F32)).astype(BF16)


def thirds(value):
    high = value.astype(BF16)
    rest = value - high.astype(F32)
    middle = rest.astype(BF16)
    return high, middle, (rest - middle.astype(F32)).astype(BF16)


def cut(value, low, high, axis):
    return lax.slice_in_dim(value, low, high, axis=axis)


def node_values(index):
    value = jnp.zeros(index.shape, F32)
    for node in range(NODES):
        value = jnp.where(index == node, math.cos(math.pi * node / (NODES - 1)) * LOG2E, value)
    return value


def z_faces(c, masks):
    n = c.shape[0]
    wrap = c[n - 1 : n] + jnp.where(masks[3], 0.0, pltpu.roll(c[0:1], 7, 1))
    closed = jnp.where(masks[3], 0.0, wrap)
    inner = c[0 : n - 1] + c[1:n]
    down = jnp.where(masks[2], c[0:1], pltpu.roll(closed, 1, 1))
    up = jnp.concatenate([inner, wrap], 0)
    return jnp.concatenate([inner, closed], 0), up + jnp.concatenate([down, inner], 0)


def z_pull(face, v):
    n = v.shape[0]
    inner, wrap = face[0 : n - 1], face[n - 1 : n]
    up = jnp.concatenate([inner * v[1:n], wrap * pltpu.roll(v[0:1], 7, 1)], 0)
    down = jnp.concatenate([pltpu.roll(wrap * v[n - 1 : n], 1, 1), inner * v[0 : n - 1]], 0)
    return up + down


class Level:
    def __init__(self, ks, c, fx, fy, fz, inv, g, e):
        self.ks, self.c, self.fx, self.fy, self.fz = ks, c, fx, fy, fz
        self.inv, self.g, self.e = inv, g, e

    def set_up(self, n, rest, masks, hide):
        ks = self.ks
        c = [self.c[(n + 1,) + rest + (k,)] for k in range(ks)]
        wrap = c[ks - 1] + jnp.where(masks[1], 0.0, pltpu.roll(c[0], 127, 2))
        closed = jnp.where(masks[1], 0.0, wrap)
        down = jnp.where(masks[0], c[0], pltpu.roll(closed, 1, 2))
        for k in range(ks):
            upper = c[k] + self.c[(n + 2,) + rest + (k,)]
            next_face = c[k] + c[k + 1] if k < ks - 1 else wrap
            z_face, z_sum = z_faces(c[k], masks)
            total = ((self.fx[(n,) + rest + (k,)] + upper) + (next_face + down)) + z_sum
            turned = pltpu.reciprocal(total, approx=True)
            for mask in hide(k):
                turned = jnp.where(mask, 0.0, turned)
            self.fx[(n + 1,) + rest + (k,)] = upper
            self.fy[(n,) + rest + (k,)] = next_face if k < ks - 1 else closed
            self.fz[(n,) + rest + (k,)] = z_face
            self.inv[(n,) + rest + (k,)] = turned
            down = next_face

    def pull(self, v, n, shift, rest):
        ks = self.ks
        f = n + shift
        last = v[(n,) + rest + (ks - 1,)]
        wrap = self.fy[(f,) + rest + (ks - 1,)]
        down = pltpu.roll(wrap * last, 1, 2)
        out = []
        for k in range(ks):
            at = rest + (k,)
            here = v[(n,) + at]
            if k < ks - 1:
                face = self.fy[(f,) + at]
                after = v[(n,) + rest + (k + 1,)]
                up = face * after
                next_down = face * here
            else:
                up = wrap * pltpu.roll(v[(n,) + rest + (0,)], 127, 2)
                next_down = None
            across = self.fx[(f,) + at] * v[(n - 1,) + at] + self.fx[(f + 1,) + at] * v[(n + 1,) + at]
            out.append((across + (up + down)) + z_pull(self.fz[(f,) + at], here))
            down = next_down
        return out

    def sweep(self, n, rest):
        moved = self.pull(self.g, n + 1, 0, rest)
        for k in range(self.ks):
            at = (n + 1,) + rest + (k,)
            self.e[(n,) + rest + (k,)] = BETA * self.g[at] + moved[k] * self.inv[at]

    def finish(self, n, rest):
        moved = self.pull(self.e, n + 1, 1, rest)
        out = []
        for k in range(self.ks):
            at = (n + 2,) + rest + (k,)
            out.append(
                (R1 * self.g[at] + R2 * self.e[(n + 1,) + rest + (k,)]) + moved[k] * self.inv[at]
            )
        return out


def kernel(
    node_f,
    node_c,
    w_f,
    w_c,
    mode_x,
    mode_y,
    mode_z,
    src_f,
    src_c,
    spread,
    gather,
    out,
    fraw,
    craw,
    nodes_f,
    nodes_c,
    weight_f,
    weight_c,
    mx,
    my_in,
    mz,
    mpad,
    xt,
    zt,
    spread_v,
    gather_v,
    mine,
    known,
    packed,
    fgot,
    fcs,
    rhs_f,
    rhs_c,
    c_f,
    fx_f,
    fy_f,
    fz_f,
    inv_f,
    g_f,
    e_f,
    c_c,
    fx_c,
    fy_c,
    fz_c,
    inv_c,
    g_c,
    e_c,
    wlane,
    qbuf,
    local_sem,
    node_send,
    node_recv,
    main_sem,
    extra_sem,
    rim_send,
    rim_recv,
):
    me_m = lax.axis_index("member")
    me_t = lax.axis_index("tile")
    parity = lax.rem(me_m, 2)
    half = me_m // 2

    def to(member, tile):
        return {"member": member, "tile": tile}

    def bring(index, source, target):
        copy = pltpu.make_async_copy(source, target, local_sem.at[index])
        copy.start()
        return copy

    own_nodes = [
        bring(0, node_f, nodes_f),
        bring(1, node_c, nodes_c),
        bring(2, w_f, weight_f),
        bring(3, w_c, weight_c),
    ]
    own_f = bring(4, src_f, fraw)
    own_c = bring(5, src_c, craw.at[:, pl.ds(8, 32)])
    modes = [
        bring(6, mode_x, mx),
        bring(7, mode_y, my_in),
        bring(8, mode_z, mz),
        bring(9, spread, spread_v),
        bring(10, gather, gather_v),
    ]

    barrier = pltpu.get_barrier_semaphore()

    def tell(device):
        pl.semaphore_signal(barrier, inc=1, device_id=device, device_id_type=MESH)

    for step in range(1, MEMBERS):
        tell(to(lax.rem(me_m + step, MEMBERS), me_t))
    aim = 4 * (half // 4) + lax.rem(half + me_t, 4)

    def aiming(strip):
        return to(2 * (4 * (me_t // 4) + lax.rem(me_t - strip + 2 * TILES, 4)) + parity, strip)

    owns = (half == me_t) & (aim == me_t)
    extra_source = half - 1 + 2 * parity
    extra_target = me_t + 1 - 2 * parity
    has_source = (extra_source >= 0) & (extra_source < TILES)
    at_home = (extra_target == half) & (aim == me_t)
    has_target = (extra_target >= 0) & (extra_target < TILES) & jnp.logical_not(at_home)
    waits_extra = has_source & jnp.logical_not(at_home)
    has_left = me_t > 0
    has_right = me_t < TILES - 1

    @pl.when(jnp.logical_not(owns))
    def _():
        tell(aiming(half))

    @pl.when(waits_extra)
    def _():
        tell(aiming(extra_source))

    @pl.when(has_left)
    def _():
        tell(to(me_m, me_t - 1))

    @pl.when(has_right)
    def _():
        tell(to(me_m, me_t + 1))

    lanes = iota((8, 128), 1)
    subs = iota((8, 128), 0)
    group = lanes & 7
    masks = (group == 0, group == 7, subs == 0, subs == 7)
    low_edge = (group == 0) & (me_t == 0)
    high_edge = (group == 7) & (me_t == TILES - 1)

    for copy in own_nodes:
        copy.wait()
    mine[...] = jnp.zeros((8, 128), F32)
    mine[0:1, 0:KL] = node_values(nodes_f[...])
    mine[1:5, 0:KL] = node_values(nodes_c[...])
    row = iota((8, 128), 0)
    weights = jnp.where(row == 0, jnp.broadcast_to(weight_f[...].astype(F32), (8, 128)), 0.0)
    for r in range(4):
        own_weight = jnp.broadcast_to(weight_c[:, r : r + 1].astype(F32), (8, 128))
        weights = jnp.where(row == r + 1, own_weight, weights)
    mine[...] = jnp.where(lanes == 15, weights, mine[...])

    def count(flag):
        return flag.astype(jnp.int32)

    pl.semaphore_wait(
        barrier,
        MEMBERS
        - count(owns)
        + count(has_target)
        + count(has_left)
        + count(has_right),
    )

    def node_copy(step):
        return pltpu.make_async_remote_copy(
            src_ref=mine,
            dst_ref=known.at[me_m],
            send_sem=node_send,
            recv_sem=node_recv,
            device_id=to(lax.rem(me_m + step, MEMBERS), me_t),
            device_id_type=MESH,
        )

    for step in range(1, MEMBERS):
        node_copy(step).start()
    known[me_m] = mine[...]

    def rim_copy(rightwards):
        if rightwards:
            return pltpu.make_async_remote_copy(
                src_ref=src_c.at[:, pl.ds(24, 8)],
                dst_ref=craw.at[:, pl.ds(0, 8)],
                send_sem=rim_send.at[0],
                recv_sem=rim_recv.at[0],
                device_id=to(me_m, lax.rem(me_t + 1, TILES)),
                device_id_type=MESH,
            )
        return pltpu.make_async_remote_copy(
            src_ref=src_c.at[:, pl.ds(0, 8)],
            dst_ref=craw.at[:, pl.ds(40, 8)],
            send_sem=rim_send.at[1],
            recv_sem=rim_recv.at[1],
            device_id=to(me_m, lax.rem(me_t + TILES - 1, TILES)),
            device_id_type=MESH,
        )

    @pl.when(has_right)
    def _():
        rim_copy(True).start()

    @pl.when(has_left)
    def _():
        rim_copy(False).start()

    craw[:, 48:64, :] = jnp.zeros((16, 16, 64), F32)

    @pl.when(jnp.logical_not(has_left))
    def _():
        craw[:, 0:8, :] = jnp.zeros((16, 8, 64), F32)

    @pl.when(jnp.logical_not(has_right))
    def _():
        craw[:, 40:48, :] = jnp.zeros((16, 8, 64), F32)

    own_f.wait()
    y = iota((512, 128), 0)
    col = iota((512, 128), 1)
    wanted = 64 * aim - 4 + KF * (col & 7) + (col >> 3)
    window = jnp.where((y == wanted) & (col < 8 * KF), 2.0, 0.0).astype(BF16)

    def pack(first, planes, at):
        high, low = halves(fraw[pl.ds(first, planes)].reshape(32 * planes, 512))
        got = jnp.dot(high, window, preferred_element_type=F32)
        got = got + jnp.dot(low, window, preferred_element_type=F32)
        packed[at : at + planes] = got.reshape(planes, 32, 128)

    pack(6 * parity, 10, 0)
    pack(14 - 14 * parity, 2, 10)

    main = pltpu.make_async_remote_copy(
        src_ref=packed.at[pl.ds(0, 10)],
        dst_ref=fgot.at[pl.ds(2 - 2 * parity, 10)],
        send_sem=main_sem.at[0],
        recv_sem=main_sem.at[1],
        device_id=to(2 * me_t + parity, aim),
        device_id_type=MESH,
    )
    extra = pltpu.make_async_remote_copy(
        src_ref=packed.at[pl.ds(10, 2)],
        dst_ref=fgot.at[pl.ds(10 * parity, 2)],
        send_sem=extra_sem.at[0],
        recv_sem=extra_sem.at[1],
        device_id=to(lax.rem(2 * extra_target + parity + MEMBERS, MEMBERS), aim),
        device_id_type=MESH,
    )

    @pl.when(jnp.logical_not(owns))
    def _():
        main.start()

    @pl.when(owns)
    def _():
        fgot[pl.ds(2 - 2 * parity, 10)] = packed[0:10]

    @pl.when(has_target)
    def _():
        extra.start()

    @pl.when(at_home)
    def _():
        fgot[pl.ds(10 * parity, 2)] = packed[10:12]

    @pl.when(jnp.logical_not(has_source))
    def _():
        fgot[pl.ds(10 * parity, 2)] = jnp.zeros((2, 32, 128), F32)

    for copy in modes:
        copy.wait()
    mpad[...] = jnp.zeros(mpad.shape, F32)
    mpad[0:KL, :] = my_in[...]
    fine_y = 64 * me_t - 4 + KF * (col & 7) + (col >> 3)
    coarse_y = 32 * me_t - 4 + KC * (col & 7) + ((col >> 3) - KF)
    picks = jnp.where(
        col < 8 * KF,
        jnp.where(y == fine_y, 1.0, 0.0),
        jnp.where(((y >> 1) == coarse_y) & (col < 8 * (KF + KC)), 0.5, 0.0),
    ).astype(BF16)
    parts = jnp.concatenate(thirds(mpad[...]), 0)
    my = jnp.dot(parts, picks, preferred_element_type=F32)
    my = (my[0:KP] + my[KP : 2 * KP]) + my[2 * KP : 3 * KP]
    own_col = iota((KP, 128), 1)
    fine_col = 64 * me_t - 4 + KF * (own_col & 7) + (own_col >> 3)
    coarse_col = 32 * me_t - 4 + KC * (own_col & 7) + ((own_col >> 3) - KF)
    reached = jnp.where(own_col < 8 * KF, fine_col, 2 * coarse_col)
    leaves = (reached < 0) | (reached >= 64 * TILES)
    my = jnp.where((iota((KP, 128), 0) == KL) & leaves, OUTSIDE, my)
    parts = jnp.concatenate(thirds(my), 0)
    wide = (KF + KC) * 128
    my = jnp.dot(parts, spread_v[:, 0:wide], preferred_element_type=F32)
    my = (my[0:KP] + my[KP : 2 * KP]) + my[2 * KP : 3 * KP]

    mpad[0:KL, 0:128] = mx[...]
    stacked = jnp.concatenate([mpad[:, 0:128]] * 8, 0)
    one = iota((XPAD, 128), 1)
    beyond = jnp.where((one == KL) | (one == KL + 1), 1.0, 0.0)
    xt[0:XPAD, :] = beyond
    xt[XPAD : XPAD + 128, :] = jnp.where(iota((128, 128), 1) == KL, 1.0, stacked.T)
    xt[XPAD + 128 : XPAD + 128 + XPAD, :] = beyond
    mpad[0:KL, 0:32] = mz[...]
    stacked = jnp.concatenate([mpad[:, 0:32]] * 8, 0)
    one = iota((32, 128), 1)
    zt[...] = jnp.where((one == KL) | (one == KL + 1), 1.0, stacked.T)
    zf = [zt[pl.ds(j, 8, stride=4), :] for j in range(4)]
    zc = [0.5 * (zf[2 * j] + zf[2 * j + 1]) for j in range(2)]
    zf = jnp.concatenate(zf, 0)
    zc = jnp.concatenate(zc, 0)

    def left(value):
        high = value.astype(BF16).astype(F32)
        return jnp.where(iota(value.shape, 1) < 32, high, value - high).astype(BF16)

    x0 = XF * me_m
    lhs_f = jnp.concatenate(
        [left(xt[pl.ds(x0 - 3 + XPAD + i, 1), :] * zf) for i in range(XF + 6)], 0
    )
    rows = []
    for i in range(XC + 6):
        at = x0 - 6 + XPAD + 2 * i
        mean = 0.5 * (xt[pl.ds(at, 1), :] + xt[pl.ds(at + 1, 1), :])
        rows.append(left(mean * zc))
    lhs_c = jnp.concatenate(rows, 0)
    rhs_f[64:128, :] = jnp.zeros((64, KF * 128), BF16)
    rhs_c[64:128, :] = jnp.zeros((64, KC * 512), BF16)

    arrivals = pltpu.make_async_remote_copy(
        src_ref=known.at[pl.ds(0, MEMBERS - 1)],
        dst_ref=known.at[pl.ds(0, MEMBERS - 1)],
        send_sem=node_send,
        recv_sem=node_recv,
        device_id=to(lax.rem(me_m + 1, MEMBERS), me_t),
        device_id_type=MESH,
    )
    arrivals.wait_recv()
    turned = known[...].reshape(128, 128).T[0:KP]
    parts = jnp.concatenate(thirds(turned), 0)
    pick = spread_v[:, wide : wide + 640]
    values = jnp.dot(parts, pick, preferred_element_type=F32)
    values = (values[0:KP] + values[KP : 2 * KP]) + values[2 * KP : 3 * KP]
    for r in range(5):
        scale = 0.125 * A3 if r == 0 else A3
        wlane[r] = jnp.broadcast_to(values[15:16, 128 * r : 128 * r + 128] * scale, (8, 128))

    def sides(value, factor):
        row = iota(value.shape, 0)
        scaled = jnp.where(row == KL, value, value * factor)
        high, low = halves(jnp.where(row == KL + 1, OUTSIDE, scaled))
        return jnp.concatenate([high, low, high, low], 0)

    for k in range(KF):
        at = slice(128 * k, 128 * k + 128)
        rhs_f[0:64, at] = sides(my[:, at], values[:, 0:128])
    for r in range(4):
        for k in range(KC):
            rhs_c[0:64, 128 * (KC * r + k) : 128 * (KC * r + k) + 128] = sides(
                my[:, 128 * (KF + k) : 128 * (KF + k) + 128],
                values[:, 128 * (r + 1) : 128 * (r + 1) + 128],
            )

    logs = jnp.dot(lhs_f, rhs_f[...], preferred_element_type=F32)
    for i in range(XF + 6):
        for k in range(KF):
            c_f[i, k] = jnp.exp2(
                logs[32 * i : 32 * i + 32, 128 * k : 128 * k + 128]
            ).reshape(4, 8, 128)
    logs = jnp.dot(lhs_c, rhs_c[...], preferred_element_type=F32)
    for i in range(XC + 6):
        for r in range(4):
            for k in range(KC):
                at = 128 * (KC * r + k)
                c_c[i, r, k] = jnp.exp2(logs[16 * i : 16 * i + 16, at : at + 128]).reshape(2, 8, 128)

    fine = Level(KF, c_f, fx_f, fy_f, fz_f, inv_f, g_f, e_f)
    coarse = Level(KC, c_c, fx_c, fy_c, fz_c, inv_c, g_c, e_c)

    def hide_fine(k):
        return ([low_edge] if k < 4 else []) + ([high_edge] if k >= 5 else [])

    def hide_coarse(k):
        return ([low_edge] if k < 4 else []) + ([high_edge] if k >= 1 else [])

    def clear(inv, planes):
        @pl.when(me_m == 0)
        def _():
            inv[0:2] = jnp.zeros((2,) + inv.shape[1:], F32)

        @pl.when(me_m == MEMBERS - 1)
        def _():
            inv[planes - 2 : planes] = jnp.zeros((2,) + inv.shape[1:], F32)

    fx_f[0] = c_f[0] + c_f[1]
    fx_c[0] = c_c[0] + c_c[1]

    def set_fine(n, carry):
        fine.set_up(n, (), masks, hide_fine)
        return carry

    lax.fori_loop(0, XF + 4, set_fine, 0)
    clear(inv_f, XF + 4)

    def set_coarse(n, carry):
        for r in range(4):
            coarse.set_up(n, (r,), masks, hide_coarse)
        return carry

    lax.fori_loop(0, XC + 4, set_coarse, 0)
    clear(inv_c, XC + 4)

    @pl.when(jnp.logical_not(owns))
    def _():
        main.wait_recv()

    @pl.when(waits_extra)
    def _():
        extra.wait_recv()

    for chunk in range(3):
        rows = []
        for i in range(4):
            for j in range(4):
                rows.append(fgot[4 * chunk + i, pl.ds(j, 8, stride=4), :])
        high, low = halves(jnp.concatenate(rows, 0))
        got = jnp.dot(high, spread_v[:, 0 : KF * 128], preferred_element_type=F32)
        got = got + jnp.dot(low, spread_v[:, 0 : KF * 128], preferred_element_type=F32)
        for i in range(4):
            n = 4 * chunk + i
            for k in range(KF):
                g_f[n, k] = (
                    got[32 * i : 32 * i + 32, 128 * k : 128 * k + 128].reshape(4, 8, 128) * inv_f[n, k]
                )

    own_c.wait()

    @pl.when(has_left)
    def _():
        rim_copy(True).wait_recv()

    @pl.when(has_right)
    def _():
        rim_copy(False).wait_recv()

    chosen = (iota((16, 64), 1) == 4 * me_m - 2 + iota((16, 64), 0)) & (iota((16, 64), 0) < 8)
    chosen = jnp.where(chosen, 1.0, 0.0).astype(BF16)
    contract = (((1,), (1,)), ((), ()))
    planes = 0.0
    for part in halves(craw[...].reshape(1024, 64)):
        planes = planes + lax.dot_general(chosen, part, contract, preferred_element_type=F32)
    rows = jnp.concatenate([planes[0:8, 128 * p : 128 * p + 128] for p in range(8)], 0)
    high, low = halves(rows)
    order = spread_v[:, wide + 640 : wide + 640 + KC * 256]
    got = jnp.dot(high, order, preferred_element_type=F32)
    got = got + jnp.dot(low, order, preferred_element_type=F32)
    for p in range(8):
        for j in range(2):
            for k in range(KC):
                at = 128 * (KC * j + k)
                fcs[pl.ds(16 * k + 8 * j + p, 8, stride=16 * KC), :] = got[
                    8 * p : 8 * p + 8, at : at + 128
                ]
    for n in range(XC + 4):
        for k in range(KC):
            at = 16 * (KC * n + k)
            source = fcs[at : at + 16, :].reshape(2, 8, 128)
            for r in range(4):
                g_c[n, r, k] = source * inv_c[n, r, k]

    def sweep_fine(n, carry):
        fine.sweep(n, ())
        return carry

    lax.fori_loop(0, XF + 2, sweep_fine, 0)

    def sweep_coarse(n, carry):
        for r in range(4):
            coarse.sweep(n, (r,))
        return carry

    lax.fori_loop(0, XC + 2, sweep_coarse, 0)

    def finish(xc, carry):
        base = pl.multiple_of(16 * xc, 16)
        low, high = fine.finish(2 * xc, ()), fine.finish(2 * xc + 1, ())
        for k in range(KF):
            pair = low[k] + high[k]
            for j in range(2):
                qbuf[pl.ds(base + 8 * j, 8), 128 * k : 128 * k + 128] = wlane[0] * (
                    pair[2 * j] + pair[2 * j + 1]
                )
        terms = [coarse.finish(xc, (r,)) for r in range(4)]
        for k in range(KC):
            at = 128 * (KF + k)
            both = (wlane[1] * terms[0][k] + wlane[2] * terms[1][k]) + (
                wlane[3] * terms[2][k] + wlane[4] * terms[3][k]
            )
            qbuf[pl.ds(base, 16), at : at + 128] = both.reshape(16, 128)
        return carry

    lax.fori_loop(0, XC, finish, 0)

    high, low = halves(qbuf[...])
    total = jnp.dot(high, gather_v[...], preferred_element_type=F32)
    total = total + jnp.dot(low, gather_v[...], preferred_element_type=F32)
    for xc in range(XC):
        for j in range(2):
            at = 16 * xc + 8 * j
            out[xc, pl.ds(j, 8, stride=2), :] = total[at : at + 8, 0:32]

    arrivals.wait_send()

    @pl.when(has_right)
    def _():
        rim_copy(True).wait_send()

    @pl.when(has_left)
    def _():
        rim_copy(False).wait_send()

    @pl.when(jnp.logical_not(owns))
    def _():
        main.wait_send()

    @pl.when(has_target)
    def _():
        extra.wait_send()


def matrices():
    lane = np.arange(128)
    group = lane % 8
    spread = np.zeros((128, 128 * (KF + KC) + 640 + 256 * KC), np.float32)
    for k in range(KF + KC):
        spread[8 * k + group, 128 * k + lane] = 1.0
    base = 128 * (KF + KC)
    for r in range(5):
        spread[8 * (lane // 8) + r, base + 128 * r + lane] = 1.0
    base += 640
    for j in range(2):
        for k in range(KC):
            spread[64 * j + 4 + KC * group + k, base + 128 * (KC * j + k) + lane] = 2.0
    gather = np.zeros((128 * (KF + KC), 32), np.float32)
    for k in range(KF + KC):
        target = (KF * group + k - 4) // 2 if k < KF else KC * group + (k - KF) - 4
        ok = (target >= 0) & (target < 32)
        gather[128 * k + lane[ok], target[ok]] = 1.0
    return jnp.asarray(spread, BF16), jnp.asarray(gather, BF16)


def body(
    node_fine,
    node_coarse,
    weight_fine,
    weight_coarse,
    mode_x,
    mode_y,
    mode_z,
    source_fine,
    source_coarse,
):
    hbm = pl.BlockSpec(memory_space=pl.ANY)
    fine = (KF, 4, 8, 128)
    coarse = (4, KC, 2, 8, 128)
    dma = pltpu.SemaphoreType.DMA

    def vmem(*shape, dtype=F32):
        return pltpu.VMEM(shape, dtype)

    wide = 128 * (KF + KC)
    scratch = [
        vmem(16, 32, 512),
        vmem(16, 64, 64),
        vmem(1, KL, dtype=jnp.int32),
        vmem(4, KL, dtype=jnp.int32),
        vmem(1, 1, dtype=jnp.int32),
        vmem(1, 4, dtype=jnp.int32),
        vmem(KL, 128),
        vmem(KL, 512),
        vmem(KL, 32),
        vmem(KP, 512),
        vmem(XPAD + 128 + XPAD, 128),
        vmem(32, 128),
        vmem(128, wide + 640 + 256 * KC, dtype=BF16),
        vmem(wide, 32, dtype=BF16),
        vmem(8, 128),
        vmem(MEMBERS, 8, 128),
        vmem(12, 32, 128),
        vmem(12, 32, 128),
        vmem(128 * KC, 128),
        vmem(128, KF * 128, dtype=BF16),
        vmem(128, KC * 512, dtype=BF16),
        vmem(XF + 6, *fine),
        vmem(XF + 5, *fine),
        vmem(XF + 4, *fine),
        vmem(XF + 4, *fine),
        vmem(XF + 4, *fine),
        vmem(XF + 4, *fine),
        vmem(XF + 2, *fine),
        vmem(XC + 6, *coarse),
        vmem(XC + 5, *coarse),
        vmem(XC + 4, *coarse),
        vmem(XC + 4, *coarse),
        vmem(XC + 4, *coarse),
        vmem(XC + 4, *coarse),
        vmem(XC + 2, *coarse),
        vmem(5, 8, 128),
        vmem(64, wide),
        dma((11,)),
        dma(()),
        dma(()),
        dma((2,)),
        dma((2,)),
        dma((2,)),
        dma((2,)),
    ]
    return pl.pallas_call(
        kernel,
        out_shape=jax.ShapeDtypeStruct((4, 16, 32), F32),
        in_specs=[hbm] * 11,
        out_specs=pl.BlockSpec(memory_space=pltpu.VMEM),
        scratch_shapes=scratch,
        compiler_params=pltpu.CompilerParams(
            collective_id=0, has_side_effects=True, vmem_limit_bytes=60 * 2**20
        ),
    )(
        node_fine,
        node_coarse,
        weight_fine.reshape(1, 1),
        weight_coarse.reshape(1, 4),
        mode_x,
        mode_y,
        mode_z,
        source_fine,
        jnp.transpose(source_coarse, (1, 2, 0)),
        *matrices(),
    )


def solution(mesh):
    return jax.shard_map(
        body,
        mesh=mesh,
        in_specs=(
            P("member", None),
            P("member", None),
            P("member"),
            P("member"),
            P(),
            P(),
            P(),
            P("tile", None, None),
            P(None, None, "tile"),
        ),
        out_specs=P("member", None, "tile"),
        check_vma=False,
    )
```

time: 248 us -> 23.7 us (0.10); the launches traced: 244 us -> 23.5 us
  local copies, waits for them, and re-layouts: 78.1 us -> 1.38 us
  waiting for transfers between devices: 75 us -> 0 us
  other arithmetic: 39.2 us -> 0 us
  starting transfers between devices: 32 us -> 0 us
  Pallas kernels: 0 us -> 21.4 us
  between operations: 14.5 us -> 0.66 us
  matrix products: 5.35 us -> 0 us
    reshape x1 -> x0, local copies, waits for them, and re-layouts: 68.4 us -> none  [restrict(): tensor.reshape(tensor.shape[0] // 2, 2, tensor.shape[1] // 2, 2, tensor.s...]
    reduce_scatter x1 -> x0, waiting for transfers between devices: 59.9 us -> none  [body(): return lax.psum_scatter(summed, 'member', scatter_dimension=0, tiled=True)]
    pallas_call x0 -> x1, Pallas kernels: none -> 21.4 us  [body(): pl.pallas_call(kernel, out_shape=jax.ShapeDtypeStruct((4, 16, 32), F32),...]
    ppermute x8 -> x0, starting transfers between devices: 21.4 us -> none  [the longest x4 16.1 us: extended(): lax.ppermute(lax.slice_in_dim(block, block.shape[dim] - width, None, axis...]
    reduce_sum x1 -> x0, other arithmetic: 20.8 us -> none  [restrict(): return blocks.sum(axis=(1, 3, 5)) * 0.125]
    add x5 -> x0, other arithmetic: 12.2 us -> none  [the longest x2 5.74 us: smooth_each(): result = result + update]
    ppermute x8 -> x0, waiting for transfers between devices: 11 us -> none  [the longest x4 11 us: extended(): lax.ppermute(lax.slice_in_dim(block, 0, width, axis=dim), axis, backward)]
    all_to_all x1 -> x0, starting transfers between devices: 10.6 us -> none  [body(): lax.all_to_all(fine_part, 'tile', split_axis=2, concat_axis=0, tiled=True)]
  transfers between devices with their start and end apart: 10 -> 0, of which waited for: 5 -> 0; matrix products, arithmetic and copies ran while one was open for 4% -> 0% of each run, Pallas kernels for 0% -> 0%
where the time goes in v4:
time: 23.7 us; the launch traced here: 23.5 us
  Pallas kernels  21.4 us (90%)
  local copies, waits for them, and re-layouts  1.38 us (6%)
  between operations  0.66 us (3%)
    pallas_call x1, Pallas kernels, body(): pl.pallas_call(kernel, out_shape=jax.ShapeDtypeStruct((4, 16, 32), F32),...  21.4 us
    unnamed x1, local copies, waits for them, and re-layouts  1.38 us

profile of v4, /device:TPU:1, one launch (start us, length us, event | category | flops | bytes accessed | tf_op | source)
XLA Modules:
  0.0 23.5 jit_solution(7346178786015126680)
XLA Ops:
  0.7 21.4 %shard_map.109 = f32[4,16,32]{2,1,0:T(8,128)} custom-call(s32[1,12]{1,0:T(1,128)} %node_f.1, s32[4,12]{1,0:T(4,128)} %node_c.1, s32[1,1]{1,0:T(1,128)} %bitcast.3.w_f, s32[1,4]{1,0:T(1,128)} %bitcast.5, f32[12,128]{1,0:T(8,128)} %mode_x.1, f32[12,512]{1,0:T(8,128)} %mode_y.1, f32[12,32]{1,0:T(8,128)} %mode_z.1, f32[16,32,512]{2,1,0:T(8,128)} %src_f.1, ...), custom_call_target="tpu_custom_call" | custom-call | tf_op jit(solution)/shard_map/pallas_call | solution.py:772
  22.1 1.4 %copy.14 = f32[4,16,32]{2,1,0:T(8,128)} copy(f32[4,16,32]{2,1,0:T(8,128)} %shard_map.109) | data formatting | bytes 16384

commit v5 on v4

--- a/solution.py
+++ b/solution.py
@@ -198,6 +198,8 @@
     fcs,
     rhs_f,
     rhs_c,
+    double_f,
+    double_c,
     c_f,
     fx_f,
     fy_f,
@@ -481,6 +483,11 @@
     rhs_f[64:128, :] = jnp.zeros((64, KF * 128), BF16)
     rhs_c[64:128, :] = jnp.zeros((64, KC * 512), BF16)
 
+    wide_end = wide + 640
+    for part in range(2):
+        double_f[128 * part : 128 * part + 128, :] = spread_v[:, 0 : KF * 128]
+        double_c[128 * part : 128 * part + 128, :] = spread_v[:, wide_end : wide_end + KC * 256]
+
     arrivals = pltpu.make_async_remote_copy(
         src_ref=known.at[pl.ds(0, MEMBERS - 1)],
         dst_ref=known.at[pl.ds(0, MEMBERS - 1)],
@@ -553,7 +560,7 @@
         fine.set_up(n, (), masks, hide_fine)
         return carry
 
-    lax.fori_loop(0, XF + 4, set_fine, 0)
+    lax.fori_loop(0, XF + 4, set_fine, 0, unroll=2)
     clear(inv_f, XF + 4)
 
     def set_coarse(n, carry):
@@ -561,7 +568,7 @@
             coarse.set_up(n, (r,), masks, hide_coarse)
         return carry
 
-    lax.fori_loop(0, XC + 4, set_coarse, 0)
+    lax.fori_loop(0, XC + 4, set_coarse, 0, unroll=2)
     clear(inv_c, XC + 4)
 
     @pl.when(jnp.logical_not(owns))
@@ -578,8 +585,9 @@
             for j in range(4):
                 rows.append(fgot[4 * chunk + i, pl.ds(j, 8, stride=4), :])
         high, low = halves(jnp.concatenate(rows, 0))
-        got = jnp.dot(high, spread_v[:, 0 : KF * 128], preferred_element_type=F32)
-        got = got + jnp.dot(low, spread_v[:, 0 : KF * 128], preferred_element_type=F32)
+        got = jnp.dot(
+            jnp.concatenate([high, low], 1), double_f[...], preferred_element_type=F32
+        )
         for i in range(4):
             n = 4 * chunk + i
             for k in range(KF):
@@ -605,9 +613,7 @@
         planes = planes + lax.dot_general(chosen, part, contract, preferred_element_type=F32)
     rows = jnp.concatenate([planes[0:8, 128 * p : 128 * p + 128] for p in range(8)], 0)
     high, low = halves(rows)
-    order = spread_v[:, wide + 640 : wide + 640 + KC * 256]
-    got = jnp.dot(high, order, preferred_element_type=F32)
-    got = got + jnp.dot(low, order, preferred_element_type=F32)
+    got = jnp.dot(jnp.concatenate([high, low], 1), double_c[...], preferred_element_type=F32)
     for p in range(8):
         for j in range(2):
             for k in range(KC):
@@ -626,14 +632,14 @@
         fine.sweep(n, ())
         return carry
 
-    lax.fori_loop(0, XF + 2, sweep_fine, 0)
+    lax.fori_loop(0, XF + 2, sweep_fine, 0, unroll=2)
 
     def sweep_coarse(n, carry):
         for r in range(4):
             coarse.sweep(n, (r,))
         return carry
 
-    lax.fori_loop(0, XC + 2, sweep_coarse, 0)
+    lax.fori_loop(0, XC + 2, sweep_coarse, 0, unroll=2)
 
     def finish(xc, carry):
         base = pl.multiple_of(16 * xc, 16)
@@ -745,6 +751,8 @@
         vmem(128 * KC, 128),
         vmem(128, KF * 128, dtype=BF16),
         vmem(128, KC * 512, dtype=BF16),
+        vmem(256, KF * 128, dtype=BF16),
+        vmem(256, KC * 256, dtype=BF16),
         vmem(XF + 6, *fine),
         vmem(XF + 5, *fine),
         vmem(XF + 4, *fine),

time: 23.7 us -> 22.1 us (0.932)
  Pallas kernels: 21.4 us -> 19.8 us
    pallas_call x1, Pallas kernels: 21.4 us -> 19.8 us  [body(): pl.pallas_call(kernel, out_shape=jax.ShapeDtypeStruct((4, 16, 32), F32),...]
where the time goes in v5:
time: 22.1 us; the launch traced here: 21.9 us
  Pallas kernels  19.8 us (90%)
  local copies, waits for them, and re-layouts  1.38 us (6%)
  between operations  0.66 us (3%)
    pallas_call x1, Pallas kernels, body(): pl.pallas_call(kernel, out_shape=jax.ShapeDtypeStruct((4, 16, 32), F32),...  19.8 us
    unnamed x1, local copies, waits for them, and re-layouts  1.38 us

profile of v5, /device:TPU:1, one launch (start us, length us, event | category | flops | bytes accessed | tf_op | source)
XLA Modules:
  0.0 21.9 jit_solution(3952956512729368214)
XLA Ops:
  0.7 19.8 %shard_map.109 = f32[4,16,32]{2,1,0:T(8,128)} custom-call(s32[1,12]{1,0:T(1,128)} %node_f.1, s32[4,12]{1,0:T(4,128)} %node_c.1, s32[1,1]{1,0:T(1,128)} %bitcast.3.w_f, s32[1,4]{1,0:T(1,128)} %bitcast.5, f32[12,128]{1,0:T(8,128)} %mode_x.1, f32[12,512]{1,0:T(8,128)} %mode_y.1, f32[12,32]{1,0:T(8,128)} %mode_z.1, f32[16,32,512]{2,1,0:T(8,128)} %src_f.1, ...), custom_call_target="tpu_custom_call" | custom-call | tf_op jit(solution)/shard_map/pallas_call | solution.py:780
  20.5 1.4 %copy.14 = f32[4,16,32]{2,1,0:T(8,128)} copy(f32[4,16,32]{2,1,0:T(8,128)} %shard_map.109) | data formatting | bytes 16384

commit v6 on v5

--- a/solution.py
+++ b/solution.py
@@ -243,6 +243,44 @@
         bring(2, w_f, weight_f),
         bring(3, w_c, weight_c),
     ]
+    barrier = pltpu.get_barrier_semaphore()
+
+    def tell(device):
+        pl.semaphore_signal(barrier, inc=1, device_id=device, device_id_type=MESH)
+
+    for step in range(1, MEMBERS):
+        tell(to(lax.rem(me_m + step, MEMBERS), me_t))
+    aim = 4 * (half // 4) + lax.rem(half + me_t, 4)
+
+    def aiming(strip):
+        return to(2 * (4 * (me_t // 4) + lax.rem(me_t - strip + 2 * TILES, 4)) + parity, strip)
+
+    owns = (half == me_t) & (aim == me_t)
+    extra_source = half - 1 + 2 * parity
+    extra_target = me_t + 1 - 2 * parity
+    has_source = (extra_source >= 0) & (extra_source < TILES)
+    at_home = (extra_target == half) & (aim == me_t)
+    has_target = (extra_target >= 0) & (extra_target < TILES) & jnp.logical_not(at_home)
+    waits_extra = has_source & jnp.logical_not(at_home)
+    has_left = me_t > 0
+    has_right = me_t < TILES - 1
+
+    @pl.when(jnp.logical_not(owns))
+    def _():
+        tell(aiming(half))
+
+    @pl.when(waits_extra)
+    def _():
+        tell(aiming(extra_source))
+
+    @pl.when(has_left)
+    def _():
+        tell(to(me_m, me_t - 1))
+
+    @pl.when(has_right)
+    def _():
+        tell(to(me_m, me_t + 1))
+
     own_f = bring(4, src_f, fraw)
     own_c = bring(5, src_c, craw.at[:, pl.ds(8, 32)])
     modes = [
@@ -252,44 +290,6 @@
         bring(9, spread, spread_v),
         bring(10, gather, gather_v),
     ]
-
-    barrier = pltpu.get_barrier_semaphore()
-
-    def tell(device):
-        pl.semaphore_signal(barrier, inc=1, device_id=device, device_id_type=MESH)
-
-    for step in range(1, MEMBERS):
-        tell(to(lax.rem(me_m + step, MEMBERS), me_t))
-    aim = 4 * (half // 4) + lax.rem(half + me_t, 4)
-
-    def aiming(strip):
-        return to(2 * (4 * (me_t // 4) + lax.rem(me_t - strip + 2 * TILES, 4)) + parity, strip)
-
-    owns = (half == me_t) & (aim == me_t)
-    extra_source = half - 1 + 2 * parity
-    extra_target = me_t + 1 - 2 * parity
-    has_source = (extra_source >= 0) & (extra_source < TILES)
-    at_home = (extra_target == half) & (aim == me_t)
-    has_target = (extra_target >= 0) & (extra_target < TILES) & jnp.logical_not(at_home)
-    waits_extra = has_source & jnp.logical_not(at_home)
-    has_left = me_t > 0
-    has_right = me_t < TILES - 1
-
-    @pl.when(jnp.logical_not(owns))
-    def _():
-        tell(aiming(half))
-
-    @pl.when(waits_extra)
-    def _():
-        tell(aiming(extra_source))
-
-    @pl.when(has_left)
-    def _():
-        tell(to(me_m, me_t - 1))
-
-    @pl.when(has_right)
-    def _():
-        tell(to(me_m, me_t + 1))
 
     lanes = iota((8, 128), 1)
     subs = iota((8, 128), 0)
@@ -560,7 +560,7 @@
         fine.set_up(n, (), masks, hide_fine)
         return carry
 
-    lax.fori_loop(0, XF + 4, set_fine, 0, unroll=2)
+    lax.fori_loop(0, XF + 4, set_fine, 0, unroll=4)
     clear(inv_f, XF + 4)
 
     def set_coarse(n, carry):
@@ -568,7 +568,7 @@
             coarse.set_up(n, (r,), masks, hide_coarse)
         return carry
 
-    lax.fori_loop(0, XC + 4, set_coarse, 0, unroll=2)
+    lax.fori_loop(0, XC + 4, set_coarse, 0, unroll=4)
     clear(inv_c, XC + 4)
 
     @pl.when(jnp.logical_not(owns))
@@ -632,7 +632,7 @@
         fine.sweep(n, ())
         return carry
 
-    lax.fori_loop(0, XF + 2, sweep_fine, 0, unroll=2)
+    lax.fori_loop(0, XF + 2, sweep_fine, 0, unroll=1)
 
     def sweep_coarse(n, carry):
         for r in range(4):
@@ -643,13 +643,18 @@
 
     def finish(xc, carry):
         base = pl.multiple_of(16 * xc, 16)
-        low, high = fine.finish(2 * xc, ()), fine.finish(2 * xc + 1, ())
+        n = 2 * xc
+        low, high = fine.pull(e_f, n + 1, 1, ()), fine.pull(e_f, n + 2, 1, ())
         for k in range(KF):
-            pair = low[k] + high[k]
+            third = low[k] * inv_f[n + 2, k] + high[k] * inv_f[n + 3, k]
+            first = g_f[n + 2, k] + g_f[n + 3, k]
+            second = e_f[n + 1, k] + e_f[n + 2, k]
             for j in range(2):
-                qbuf[pl.ds(base + 8 * j, 8), 128 * k : 128 * k + 128] = wlane[0] * (
-                    pair[2 * j] + pair[2 * j + 1]
-                )
+                at = (2 * j, 2 * j + 1)
+                total = (
+                    R1 * (first[at[0]] + first[at[1]]) + R2 * (second[at[0]] + second[at[1]])
+                ) + (third[at[0]] + third[at[1]])
+                qbuf[pl.ds(base + 8 * j, 8), 128 * k : 128 * k + 128] = wlane[0] * total
         terms = [coarse.finish(xc, (r,)) for r in range(4)]
         for k in range(KC):
             at = 128 * (KF + k)

time: 22.1 us -> 22 us (level)
    pallas_call x1, Pallas kernels: 19.8 us -> 19.6 us  [body(): pl.pallas_call(kernel, out_shape=jax.ShapeDtypeStruct((4, 16, 32), F32),...]
where the time goes in v6:
time: 22 us; the launch traced here: 21.6 us
  Pallas kernels  19.6 us (89%)
  local copies, waits for them, and re-layouts  1.38 us (6%)
  between operations  0.66 us (3%)
    pallas_call x1, Pallas kernels, body(): pl.pallas_call(kernel, out_shape=jax.ShapeDtypeStruct((4, 16, 32), F32),...  19.6 us
    unnamed x1, local copies, waits for them, and re-layouts  1.38 us

profile of v6, /device:TPU:1, one launch (start us, length us, event | category | flops | bytes accessed | tf_op | source)
XLA Modules:
  0.0 21.6 jit_solution(7687868018807483322)
XLA Ops:
  0.7 19.6 %shard_map.109 = f32[4,16,32]{2,1,0:T(8,128)} custom-call(s32[1,12]{1,0:T(1,128)} %node_f.1, s32[4,12]{1,0:T(4,128)} %node_c.1, s32[1,1]{1,0:T(1,128)} %bitcast.3.w_f, s32[1,4]{1,0:T(1,128)} %bitcast.5, f32[12,128]{1,0:T(8,128)} %mode_x.1, f32[12,512]{1,0:T(8,128)} %mode_y.1, f32[12,32]{1,0:T(8,128)} %mode_z.1, f32[16,32,512]{2,1,0:T(8,128)} %src_f.1, ...), custom_call_target="tpu_custom_call" | custom-call | tf_op jit(solution)/shard_map/pallas_call | solution.py:785
  20.2 1.4 %copy.14 = f32[4,16,32]{2,1,0:T(8,128)} copy(f32[4,16,32]{2,1,0:T(8,128)} %shard_map.109) | data formatting | bytes 16384
